TPU v7x, 32 devices: a whole 2x2x4 slice. The times are simulated.
32 devices in a mesh: frame: 16 (over z, y, x), space: 2 (over core).
Axes of the slice: x: 2, y: 2, z: 4, core: 2. Of those that a mesh axis runs over, the one named last changes fastest.
Arguments:
- block_input: bfloat16 [2, 4096, 768], P(None, ('frame', 'space')), may hold values from -6 to 6
- norm1_gain: float32 [768], replicated, may hold values from 0.5 to 1.5
- w_query: bfloat16 [768, 768], replicated, may hold values from -0.3125 to 0.3125
- w_key: bfloat16 [768, 768], replicated, may hold values from -0.3125 to 0.3125
- w_value: bfloat16 [768, 768], replicated, may hold values from -0.21875 to 0.21875
- w_out: bfloat16 [768, 768], replicated, may hold values from -1.75 to 1.75
- norm2_gain: float32 [768], replicated, may hold values from 0.5 to 1.5
- w_up: bfloat16 [768, 3072], replicated, may hold values from -0.21875 to 0.21875
- w_down: bfloat16 [3072, 768], replicated, may hold values from -0.109375 to 0.109375
- clip_frames: int32 [2, 4], replicated, may hold values from 0 to 16, as said below
- cotangent: bfloat16 [2, 4096, 768], P(None, ('frame', 'space')), may hold values from -6 to 6
Outputs:
- block_output: bfloat16 [2, 4096, 768], P(None, ('frame', 'space'))
- grad_input: float32 [2, 4096, 768], P(None, ('frame', 'space'))
- grad_norm1_gain: float32 [768], replicated
- grad_w_query: float32 [768, 768], replicated
- grad_w_key: float32 [768, 768], replicated
- grad_w_value: float32 [768, 768], replicated
- grad_w_out: float32 [768, 768], replicated
- grad_norm2_gain: float32 [768], replicated
- grad_w_up: float32 [768, 3072], replicated
- grad_w_down: float32 [3072, 768], replicated
Inputs may be any that keep to these rules, and one draw needn't show every extreme that they name: `clip_frames`: row s lists the lengths in frames of stream s's clips in order; each row sums to 16; a length is 0 or a multiple of 4, and zeros come only after the last clip; in one stream, drawn from the seed, a single clip holds all 16 frames.
All inputs are finite; a program needn't handle non-finite values.
Results may differ from a plain program's by a relative error of at most 0.017.
Values may be sent and summed in bfloat16 or wider, within the bound.
No kernel may reach another device: no remote copies, remote signals or barrier semaphores. Data moves between devices by JAX's collectives and lax.ppermute only.
A program may use at most 320 MiB of HBM per device.

v0:
```python
import math

import jax
import jax.numpy as jnp
import numpy as np
from jax import lax
from jax.experimental import pallas as pl
from jax.experimental.pallas import tpu as pltpu
from jax.sharding import PartitionSpec as P

HEADS = 12
HEAD_DIM = 64
VMEM = pl.BlockSpec(memory_space=pltpu.VMEM)
SMEM = pl.BlockSpec(memory_space=pltpu.SMEM)
LIMIT = pltpu.CompilerParams(vmem_limit_bytes=56 * 2**20)
CLIP = 4


def dot(left, right, left_dim, right_dim):
    return lax.dot_general(
        left,
        right,
        (((left_dim,), (right_dim,)), ((), ())),
        preferred_element_type=jnp.float32,
    )


def head_owners(frames, spaces):
    planes = frames // 4
    share = -(-HEADS // planes)
    return [
        [
            ((head // share) * 4 + (head % share) // spaces * 2 + stream) * spaces
            + (head % share) % spaces
            for head in range(HEADS)
        ]
        for stream in range(2)
    ]


def normalize(values):
    average = jnp.mean(values, axis=-1, keepdims=True)
    centred = values - average
    root = lax.rsqrt(jnp.mean(centred * centred, axis=-1, keepdims=True) + 1e-05)
    return centred * root, root


def normalize_back(d_scaled, unit, root, gain):
    d_unit = d_scaled * gain
    mean_one = jnp.mean(d_unit, axis=-1, keepdims=True)
    mean_two = jnp.mean(d_unit * unit, axis=-1, keepdims=True)
    return root * (d_unit - mean_one - unit * mean_two)


def frequencies(columns):
    half = HEAD_DIM // 2
    values = np.exp(np.arange(half) * (-2.0 * math.log(10000.0) / HEAD_DIM))
    return jnp.asarray(np.broadcast_to(values[:, None], (half, columns)), jnp.float32)


def turned(value, cosine, sine, sign):
    half = HEAD_DIM // 2
    first, second = value[:half], value[half:]
    return jnp.concatenate(
        [first * cosine - sign * second * sine, second * cosine + sign * first * sine], axis=0
    )


def project(place, clips, block_input, gain, w_query, w_key, w_value, owners, devices, per_frame):
    streams, rows, width = block_input.shape
    half = HEAD_DIM // 2
    low = jnp.bfloat16
    scale = 1.0 / math.sqrt(HEAD_DIM)
    owned = {device for row in owners for device in row}

    def body(place_ref, clips_ref, freq_ref, x_ref, gain_ref, wq, wk, wv, out, normed_out, table):
        frame, first_row = place_ref[0], place_ref[1]
        for stream in range(streams):
            begin = jnp.int32(0)
            running = jnp.int32(0)
            for clip in range(clips_ref.shape[1]):
                length = clips_ref[stream, clip]
                begin = jnp.where((frame >= running) & (frame < running + length), running, begin)
                running = running + length
            row = lax.broadcasted_iota(jnp.int32, (half, rows), 1)
            position = ((frame - begin) * per_frame + first_row + row).astype(jnp.float32)
            angles = position * freq_ref[...]
            table[0, stream] = jnp.cos(angles)
            table[1, stream] = jnp.sin(angles)
        values = x_ref[...].astype(jnp.float32).reshape(streams * rows, width)
        normed = (normalize(values)[0] * gain_ref[...]).astype(low)
        normed_out[...] = normed.reshape(streams, rows, width)
        for kind, weight in enumerate((wq, wk, wv)):
            product = dot(normed, weight[...], 1, 0).T
            for stream in range(streams):
                columns = slice(stream * rows, (stream + 1) * rows)
                for head in range(HEADS):
                    piece = product[head * HEAD_DIM : (head + 1) * HEAD_DIM, columns]
                    if kind < 2:
                        piece = turned(piece, table[0, stream], table[1, stream], 1.0)
                    if kind == 0:
                        piece = piece * scale
                    out[
                        owners[stream][head], kind * HEAD_DIM : (kind + 1) * HEAD_DIM, :
                    ] = piece.astype(low)
        for spare in range(devices):
            if spare not in owned:
                out[spare] = jnp.zeros((3 * HEAD_DIM, rows), low)

    return pl.pallas_call(
        body,
        out_shape=(
            jax.ShapeDtypeStruct((devices, 3 * HEAD_DIM, rows), low),
            jax.ShapeDtypeStruct((streams, rows, width), low),
        ),
        in_specs=[SMEM, SMEM] + [VMEM] * 6,
        out_specs=(VMEM, VMEM),
        scratch_shapes=[pltpu.VMEM((2, streams, half, rows), jnp.float32)],
        compiler_params=LIMIT,
        name="project",
    )(place, clips, frequencies(rows), block_input, gain[None, :], w_query, w_key, w_value)


def rope_tables(lo, frames, per_frame):
    half = HEAD_DIM // 2

    def body(lo_ref, freq_ref, out):
        def one(frame, _):
            row = lax.broadcasted_iota(jnp.int32, (half, per_frame), 1)
            position = ((frame - lo_ref[frame]) * per_frame + row).astype(jnp.float32)
            angles = position * freq_ref[...]
            out[frame, 0] = jnp.cos(angles)
            out[frame, 1] = jnp.sin(angles)
            return 0

        lax.fori_loop(0, frames, one, 0)

    return pl.pallas_call(
        body,
        out_shape=jax.ShapeDtypeStruct((frames, 2, half, per_frame), jnp.float32),
        in_specs=[SMEM, VMEM],
        out_specs=VMEM,
        compiler_params=LIMIT,
        name="rope_tables",
    )(lo, frequencies(per_frame))


GELU = math.sqrt(2.0 / math.pi)


def gelu_pair(value):
    square = value * value
    bent = jnp.tanh(GELU * value * (1.0 + 0.044715 * square))
    side = 0.5 * (1.0 + bent)
    slope = side + 0.5 * value * (1.0 - bent * bent) * (GELU * (1.0 + 3 * 0.044715 * square))
    return value * side, slope


def attention_out(attended, block_input, w_out, gain, owners):
    streams, rows, width = block_input.shape
    low = jnp.bfloat16

    def body(att, x_ref, wo, gain_ref, middle, two_ref):
        for stream in range(streams):
            rows_of = slice(stream * rows, (stream + 1) * rows)
            flat = jnp.concatenate([att[owner] for owner in owners[stream]], axis=0)
            values = x_ref[stream].astype(jnp.float32) + dot(flat.T, wo[...], 1, 0)
            middle[rows_of] = values
            two_ref[rows_of] = (normalize(values)[0] * gain_ref[...]).astype(low)

    return pl.pallas_call(
        body,
        out_shape=(
            jax.ShapeDtypeStruct((streams * rows, width), jnp.float32),
            jax.ShapeDtypeStruct((streams * rows, width), low),
        ),
        in_specs=[VMEM] * 4,
        out_specs=(VMEM, VMEM),
        compiler_params=LIMIT,
        name="attention_out",
    )(attended, block_input, w_out, gain[None, :])


def whole(shape):
    return pl.BlockSpec(shape, lambda *indices: (0,) * len(shape))


def feed_first(two, cotangent, w_up, w_down, chunk, steps):
    tokens, width = two.shape
    low = jnp.bfloat16

    def body(two_ref, cot, up, down, result, d_two):
        cot_flat = cot[...].reshape(tokens, width)
        active, slope = gelu_pair(dot(two_ref[...], up[...], 1, 0))
        d_hidden = (dot(cot_flat, down[...], 1, 1) * slope).astype(low)
        forward = dot(active.astype(low), down[...], 1, 0)
        backward = dot(d_hidden, up[...], 1, 1)

        @pl.when(pl.program_id(0) == 0)
        def _():
            result[...] = forward
            d_two[...] = backward

        @pl.when(pl.program_id(0) > 0)
        def _():
            result[...] += forward
            d_two[...] += backward

    return pl.pallas_call(
        body,
        grid=(steps,),
        out_shape=(jax.ShapeDtypeStruct((tokens, width), jnp.float32),) * 2,
        in_specs=[
            whole(two.shape), whole(cotangent.shape),
            pl.BlockSpec((width, chunk), lambda i: (0, i)),
            pl.BlockSpec((chunk, width), lambda i: (i, 0)),
        ],
        out_specs=(whole((tokens, width)),) * 2,
        compiler_params=LIMIT,
        name="feed_first",
    )(two, cotangent, w_up, w_down)


def feed_rest(core, so_far, attended, middle, two, cotangent, w_out, gain, w_up, w_down, chunk, skip, owners):
    devices, head_width, rows = attended.shape
    streams, _, width = cotangent.shape
    tokens = streams * rows
    half = width // 2
    steps = w_up.shape[1] // chunk - skip
    low = jnp.bfloat16
    f32 = jnp.float32
    owned = {device for row in owners for device in row}

    def body(
        core_ref, first_result, first_two, att, middle, two_ref, cot, wo, gain_ref, up, down,
        result_ref, d_middle_ref, d_own, keep, give,
        result, d_two,
    ):
        step = pl.program_id(0)
        cot_flat = cot[...].reshape(tokens, width)
        active, slope = gelu_pair(dot(two_ref[...], up[...], 1, 0))
        d_hidden = (dot(cot_flat, down[...], 1, 1) * slope).astype(low)
        forward = dot(active.astype(low), down[...], 1, 0)
        backward = dot(d_hidden, up[...], 1, 1)

        @pl.when(step == 0)
        def _():
            result[...] = first_result[...] + forward
            d_two[...] = first_two[...] + backward

        @pl.when(step > 0)
        def _():
            result[...] += forward
            d_two[...] += backward

        @pl.when(step == steps - 1)
        def _():
            result_ref[...] = (middle[...] + result[...]).astype(low).reshape(streams, rows, width)
            unit, root = normalize(middle[...])
            d_middle = cot_flat.astype(f32) + normalize_back(
                d_two[...], unit, root, gain_ref[...]
            )
            d_middle_ref[...] = d_middle
            branch = d_middle.astype(low)
            d_att = dot(branch, wo[...], 1, 1).T.astype(low)
            total = jnp.zeros((width, width), f32)
            for stream in range(streams):
                rows_of = slice(stream * rows, (stream + 1) * rows)
                for head, owner in enumerate(owners[stream]):
                    d_own[owner] = d_att[head * HEAD_DIM : (head + 1) * HEAD_DIM, rows_of]
                flat = jnp.concatenate([att[owner] for owner in owners[stream]], axis=0)
                total += dot(flat, branch[rows_of], 1, 0)
            for spare in range(devices):
                if spare not in owned:
                    d_own[spare] = jnp.zeros((head_width, rows), low)
            first = core_ref[0] == 0
            keep[...] = jnp.where(first, total[:, :half], total[:, half:])
            give[...] = jnp.where(first, total[:, half:], total[:, :half]).astype(low)

    shapes = (
        ((streams, rows, width), low),
        ((tokens, width), f32),
        ((devices, head_width, rows), low),
        ((width, half), f32),
        ((width, half), low),
    )
    return pl.pallas_call(
        body,
        grid=(steps,),
        out_shape=tuple(jax.ShapeDtypeStruct(*entry) for entry in shapes),
        in_specs=[
            SMEM, whole((tokens, width)), whole((tokens, width)),
            whole(attended.shape), whole(middle.shape), whole(two.shape),
            whole(cotangent.shape), whole(w_out.shape), whole((1, width)),
            pl.BlockSpec((width, chunk), lambda i: (0, i + skip)),
            pl.BlockSpec((chunk, width), lambda i: (i + skip, 0)),
        ],
        out_specs=tuple(whole(shape) for shape, _ in shapes),
        scratch_shapes=[pltpu.VMEM((tokens, width), f32), pltpu.VMEM((tokens, width), f32)],
        compiler_params=LIMIT,
        name="feed_rest",
    )(core, *so_far, attended, middle, two, cotangent, w_out, gain[None, :], w_up, w_down)


def out_rows(width, planes):
    return -(-(width // 4) // (16 * planes)) * 16


def hidden_gradients(
    where, two_mine, two_other, cot_mine, cot_other, w_up, w_down, out_quarter, slots, planes
):
    pieces, tokens, width = two_mine.shape
    hidden = w_up.shape[1] // slots
    rows = width // planes
    extra = out_rows(width, planes)
    quarter = out_quarter.shape[0]
    height = 2 * rows + extra
    low = jnp.bfloat16

    def body(where_ref, two_a, two_b, cot_a, cot_b, up, down, quarter_ref, *rest):
        outs, (up_sum, down_sum, out_sum) = rest[:planes], rest[planes:]
        step = pl.program_id(0)

        def run(two, cot):
            active, slope = gelu_pair(dot(two, up[...], 1, 0))
            d_hidden = (dot(cot, down[...], 1, 1) * slope).astype(low)
            up_term = dot(two, d_hidden, 0, 0)
            down_term = dot(active.astype(low), cot, 0, 0)

            @pl.when(step == 0)
            def _():
                up_sum[...] = up_term
                down_sum[:hidden] = down_term[:, :hidden]
                down_sum[hidden:] = down_term[:, hidden:]

            @pl.when(step > 0)
            def _():
                up_sum[...] += up_term
                down_sum[:hidden] += down_term[:, :hidden]
                down_sum[hidden:] += down_term[:, hidden:]

        @pl.when(step < pieces // 2)
        def _():
            run(two_a[...].reshape(2 * tokens, width), cot_a[...].reshape(2 * tokens, width))

        @pl.when(step >= pieces // 2)
        def _():
            run(two_b[...].reshape(2 * tokens, width), cot_b[...].reshape(2 * tokens, width))

        @pl.when(step == pieces - 1)
        def _():
            out_sum[...] = jnp.zeros_like(out_sum)
            out_sum[:quarter] = quarter_ref[...]
            for index, out in enumerate(outs):
                plane = lax.rem(where_ref[1] + index, planes)
                rows_of = pl.ds(pl.multiple_of(plane * rows, rows), rows)
                out[:rows] = up_sum[rows_of, :].astype(low)
                out[rows : 2 * rows] = down_sum[rows_of, :].astype(low)
                out[2 * rows :] = out_sum[
                    pl.ds(pl.multiple_of(plane * extra, extra), extra), :
                ].astype(low)

    near = pl.BlockSpec(
        (2, tokens, width), lambda i, where: (jnp.minimum(i, pieces // 2 - 1), 0, 0)
    )
    far = pl.BlockSpec((2, tokens, width), lambda i, where: (jnp.maximum(i - pieces // 2, 0), 0, 0))
    return pl.pallas_call(
        body,
        grid_spec=pltpu.PrefetchScalarGridSpec(
            num_scalar_prefetch=1,
            grid=(pieces,),
            in_specs=[
                near, far, near, far,
                pl.BlockSpec((width, hidden), lambda i, where: (0, where[0])),
                pl.BlockSpec((hidden, width), lambda i, where: (where[0], 0)),
                whole(out_quarter.shape),
            ],
            out_specs=[whole((height, hidden))] * planes,
            scratch_shapes=[
                pltpu.VMEM((width, hidden), jnp.float32),
                pltpu.VMEM((width, hidden), jnp.float32),
                pltpu.VMEM((extra * planes, hidden), jnp.float32),
            ],
        ),
        out_shape=[jax.ShapeDtypeStruct((height, hidden), low)] * planes,
        compiler_params=LIMIT,
        name="hidden_gradients",
    )(where, two_mine, two_other, cot_mine, cot_other, w_up, w_down, out_quarter)


def place_hidden(where, mine, other, w_up, w_out, gain, slots):
    spots, planes, height, hidden = mine.shape
    width = w_up.shape[0]
    rows = width // planes
    extra = out_rows(width, planes)
    quarter = width // 4
    f32 = jnp.float32

    def body(where_ref, mine_ref, other_ref, up_ref, gain_ref, up_out, down_out, out, gain_out, low):
        step = pl.program_id(0)

        def put(ref):
            for index in range(planes):
                plane = lax.rem(where_ref[3, 0] + planes - index, planes)
                rows_of = pl.ds(pl.multiple_of(plane * rows, rows), rows)
                up_out[rows_of, :] = ref[0, index, :rows].astype(f32)
                low[rows_of, :] = ref[0, index, rows : 2 * rows].astype(f32)
                row = where_ref[1, step] * quarter + plane * extra
                rows_of = pl.ds(pl.multiple_of(row, 16), extra)
                piece = ref[0, index, 2 * rows :].astype(f32)

                @pl.when((plane * extra < quarter) & (where_ref[2, step] == 0))
                def _():
                    out[rows_of, :hidden] = piece

                @pl.when((plane * extra < quarter) & (where_ref[2, step] == 1))
                def _():
                    out[rows_of, hidden:] = piece

        @pl.when(step < spots)
        def _():
            put(mine_ref)

        @pl.when(step >= spots)
        def _():
            put(other_ref)

        down_out[:, :hidden] = low[:hidden]
        down_out[:, hidden:] = low[hidden:]
        terms = jnp.sum(up_out[...] * up_ref[...].astype(f32), axis=1, keepdims=True)

        @pl.when(step == 0)
        def _():
            gain_out[...] = terms

        @pl.when(step > 0)
        def _():
            gain_out[...] += terms

        @pl.when(step == slots - 1)
        def _():
            gain_out[...] /= gain_ref[...]

    return pl.pallas_call(
        body,
        grid_spec=pltpu.PrefetchScalarGridSpec(
            num_scalar_prefetch=1,
            grid=(slots,),
            in_specs=[
                pl.BlockSpec(
                    (1, planes, height, hidden),
                    lambda i, where: (jnp.minimum(i, spots - 1), 0, 0, 0),
                ),
                pl.BlockSpec(
                    (1, planes, height, hidden),
                    lambda i, where: (jnp.maximum(i - spots, 0), 0, 0, 0),
                ),
                pl.BlockSpec((width, hidden), lambda i, where: (0, where[0, i])),
                whole((width, 1)),
            ],
            out_specs=[
                pl.BlockSpec((width, hidden), lambda i, where: (0, where[0, i])),
                pl.BlockSpec((hidden, width), lambda i, where: (where[0, i], 0)),
                whole((width, width)),
                whole((width, 1)),
            ],
            scratch_shapes=[pltpu.VMEM((width, hidden), f32)],
        ),
        out_shape=[
            jax.ShapeDtypeStruct(w_up.shape, f32),
            jax.ShapeDtypeStruct(w_up.shape[::-1], f32),
            jax.ShapeDtypeStruct(w_out.shape, f32),
            jax.ShapeDtypeStruct((width, 1), f32),
        ],
        compiler_params=LIMIT,
        name="place_hidden",
    )(where, mine, other, w_up, gain[:, None])


def head_products(where, grads, mine, other):
    devices, height, rows = grads.shape
    frames, _, width = mine.shape
    half = width // 2

    def body(where_ref, d_ref, a_ref, b_ref, keep, give, total):
        core = where_ref[0]
        total[...] = jnp.zeros_like(total)

        def one(pair, _):
            lefts, rights = [], []
            for frame in (2 * pair, 2 * pair + 1):
                lefts += [d_ref[2 * frame + core], d_ref[2 * frame + 1 - core]]
                rights += [a_ref[frame], b_ref[frame]]
            total[...] += dot(
                jnp.concatenate(lefts, axis=1), jnp.concatenate(rights, axis=0), 1, 0
            )
            return 0

        lax.fori_loop(0, frames // 2, one, 0)
        first = where_ref[1] == 0
        keep[...] = jnp.where(first, total[:, :half], total[:, half:])
        give[...] = jnp.where(first, total[:, half:], total[:, :half]).astype(jnp.bfloat16)

    return pl.pallas_call(
        body,
        out_shape=(
            jax.ShapeDtypeStruct((height, half), jnp.float32),
            jax.ShapeDtypeStruct((height, half), jnp.bfloat16),
        ),
        in_specs=[SMEM] + [VMEM] * 3,
        out_specs=(VMEM, VMEM),
        scratch_shapes=[pltpu.VMEM((height, width), jnp.float32)],
        compiler_params=LIMIT,
        name="head_products",
    )(where, grads, mine, other)


def place_heads(where, mine, other, weights, gain, owners):
    _, height, half = mine.shape
    width = 2 * half
    f32 = jnp.float32

    def body(where_ref, mine_ref, other_ref, wq, wk, wv, gain_ref, dq, dk, dv, gain_out):
        for side in range(2):
            blocks = []
            for head in range(HEADS):
                entry = where_ref[side, head]
                own = where_ref[2, 0] == owners[0][head] % 2
                blocks.append(jnp.where(own, mine_ref[entry], other_ref[entry]))
            rows_of = slice(side * half, (side + 1) * half)
            terms = jnp.zeros((half, 1), f32)
            for kind, (weight, out) in enumerate(((wq, dq), (wk, dk), (wv, dv))):
                rows = slice(kind * HEAD_DIM, (kind + 1) * HEAD_DIM)
                flat = jnp.concatenate([block[rows] for block in blocks], axis=0)
                grad = flat.T.astype(f32)
                out[rows_of] = grad
                terms += jnp.sum(grad * weight[rows_of].astype(f32), axis=1, keepdims=True)
            gain_out[rows_of] = terms / gain_ref[rows_of]

    return pl.pallas_call(
        body,
        out_shape=[jax.ShapeDtypeStruct((width, width), f32)] * 3
        + [jax.ShapeDtypeStruct((width, 1), f32)],
        in_specs=[SMEM] + [VMEM] * 6,
        out_specs=[VMEM] * 4,
        compiler_params=LIMIT,
        name="place_heads",
    )(where, mine, other, *weights, gain[:, None])


def input_gradient(grads, weights, block_input, gain, d_middle, owners):
    streams, rows, width = block_input.shape

    def body(d_ref, wq, wk, wv, x_ref, gain_ref, d_middle_ref, out):
        for stream in range(streams):
            d_normed = jnp.zeros((rows, width), jnp.float32)
            for kind, weight in enumerate((wq, wk, wv)):
                rows_of = slice(kind * HEAD_DIM, (kind + 1) * HEAD_DIM)
                flat = jnp.concatenate([d_ref[owner, rows_of] for owner in owners[stream]], axis=0)
                d_normed += dot(flat.T, weight[...], 1, 1)
            unit, root = normalize(x_ref[stream].astype(jnp.float32))
            d_values = normalize_back(d_normed, unit, root, gain_ref[...])
            out[stream] = d_middle_ref[stream * rows : (stream + 1) * rows] + d_values

    return pl.pallas_call(
        body,
        out_shape=jax.ShapeDtypeStruct(block_input.shape, jnp.float32),
        in_specs=[VMEM] * 7,
        out_specs=VMEM,
        compiler_params=LIMIT,
        name="input_gradient",
    )(grads, *weights, block_input, gain[None, :], d_middle)


def wide(ref, frame, spaces, first, last, count=1):
    return jnp.concatenate(
        [ref[frame * spaces + j, first:last, :] for j in range(spaces * count)], axis=1
    )


def attend(lo, packed, frames):
    devices, _, rows = packed.shape
    spaces = devices // frames
    per_frame = rows * spaces
    dim = HEAD_DIM

    def body(lo_ref, r_ref, o_ref, low_ref, lse_ref, kv, top, total, summed):
        def turn_keys(device, _):
            kv[pl.ds(pl.multiple_of(device * rows, rows), rows), :] = r_ref[device, dim:, :].T
            return 0

        lax.fori_loop(0, devices, turn_keys, 0, unroll=4)

        def group(queries, _):
            first = queries * CLIP
            query = [wide(r_ref, first + i, spaces, 0, dim) for i in range(CLIP)]

            def update(i, keys, count, fresh):
                base = pl.multiple_of(keys * CLIP * per_frame, per_frame)
                scores = dot(kv[pl.ds(base, count * per_frame), :dim], query[i], 1, 0)
                new_top = jnp.max(scores, axis=0, keepdims=True)
                if not fresh:
                    old_top = top[i]
                    new_top = jnp.maximum(old_top, new_top)
                weights = jnp.exp(scores - new_top)
                new_total = jnp.sum(weights, axis=0, keepdims=True)
                values = wide(r_ref, keys * CLIP, spaces, 2 * dim, 3 * dim, count)
                new_sum = dot(values, weights.astype(jnp.bfloat16), 1, 0)
                if not fresh:
                    factor = jnp.exp(old_top - new_top)
                    new_total += total[i] * factor
                    new_sum += summed[i] * factor
                top[i] = new_top
                total[i] = new_total
                summed[i] = new_sum

            for i in range(CLIP):
                update(i, queries, i + 1, True)

            def earlier(keys, _):
                for i in range(CLIP):
                    update(i, keys, CLIP, False)
                return 0

            lax.fori_loop(lo_ref[first] // CLIP, queries, earlier, 0)
            for i in range(CLIP):
                out = summed[i] / total[i]
                for j in range(spaces):
                    piece = out[:, j * rows : (j + 1) * rows]
                    o_ref[(first + i) * spaces + j] = piece
                    low_ref[(first + i) * spaces + j] = piece.astype(jnp.bfloat16)
                lse_ref[first + i] = top[i] + jnp.log(total[i])
            return 0

        lax.fori_loop(0, frames // CLIP, group, 0)

    f32 = jnp.float32
    return pl.pallas_call(
        body,
        out_shape=(
            jax.ShapeDtypeStruct((devices, dim, rows), f32),
            jax.ShapeDtypeStruct((devices, dim, rows), jnp.bfloat16),
            jax.ShapeDtypeStruct((frames, 1, per_frame), f32),
            jax.ShapeDtypeStruct((devices * rows, 2 * dim), jnp.bfloat16),
        ),
        in_specs=[SMEM, VMEM],
        out_specs=(VMEM,) * 4,
        scratch_shapes=[
            pltpu.VMEM((CLIP, 1, per_frame), f32),
            pltpu.VMEM((CLIP, 1, per_frame), f32),
            pltpu.VMEM((CLIP, dim, per_frame), f32),
        ],
        compiler_params=LIMIT,
        name="attend",
    )(lo, packed)


def attend_back_ready(packed, d_own, out, frames):
    devices, _, rows = packed.shape
    spaces = devices // frames
    dim = HEAD_DIM

    def body(r_ref, d_ref, o_ref, qd, delta):
        def turn_frame(frame, _):
            for j in range(spaces):
                device = frame * spaces + j
                both = jnp.concatenate([r_ref[device, :dim, :], d_ref[device]], axis=0)
                qd[pl.ds(pl.multiple_of(device * rows, rows), rows), :] = both.T
                delta[frame, :, j * rows : (j + 1) * rows] = jnp.sum(
                    d_ref[device].astype(jnp.float32) * o_ref[device], axis=0, keepdims=True
                )
            return 0

        lax.fori_loop(0, frames, turn_frame, 0, unroll=2)

    return pl.pallas_call(
        body,
        out_shape=(
            jax.ShapeDtypeStruct((devices * rows, 2 * dim), jnp.bfloat16),
            jax.ShapeDtypeStruct((frames, 1, spaces * rows), jnp.float32),
        ),
        in_specs=[VMEM] * 3,
        out_specs=(VMEM, VMEM),
        compiler_params=LIMIT,
        name="attend_back_ready",
    )(packed, d_own, out)


def attend_back(hi, packed, d_own, lse, delta, kv, qd, tables, d_query, earlier, frames, start, stop):
    devices, _, rows = packed.shape
    spaces = devices // frames
    per_frame = rows * spaces
    dim = HEAD_DIM
    last = stop * CLIP == frames
    f32 = jnp.float32
    shift = dim if last else 0
    base = 0 if last else start * CLIP * spaces

    def body(hi_ref, r_ref, d_ref, lse_ref, delta_ref, kv_ref, qd_ref, table_ref, *rest):
        rest = list(rest)
        before = rest.pop(0) if start else None
        pieces = [rest.pop(0) for _ in earlier] if last else []
        out = rest.pop(0)
        d_query_ref, acc, left = rest

        def begin(frame, _):
            d_query_ref[frame] = before[frame] if start else jnp.zeros((dim, per_frame), f32)
            return 0

        lax.fori_loop(0, frames, begin, 0)
        done = 0
        for piece in pieces:
            out[done : done + piece.shape[0], dim:, :] = piece[...]
            done += piece.shape[0]
        first_half = lax.broadcasted_iota(jnp.int32, (per_frame, 2 * dim), 1) < dim

        def group(keys, _):
            first = keys * CLIP
            for i in range(CLIP):
                rows_of = pl.ds(pl.multiple_of((first + i) * per_frame, per_frame), per_frame)
                both = kv_ref[rows_of, :]
                zero = jnp.zeros_like(both)
                left[i, :per_frame] = jnp.where(first_half, both, zero)
                left[i, per_frame:] = jnp.where(first_half, zero, both)

            def block(i, frame, count, fresh):
                own = [d_ref[frame * spaces + j] for j in range(spaces * count)]
                right = jnp.concatenate(
                    [wide(r_ref, frame, spaces, 0, dim, count), jnp.concatenate(own, axis=1)],
                    axis=0,
                )
                both = dot(left[i], right, 1, 0)
                row = lambda ref: jnp.concatenate([ref[frame + j] for j in range(count)], axis=1)
                weights = jnp.exp(both[:per_frame] - row(lse_ref))
                d_scores = (weights * (both[per_frame:] - row(delta_ref))).astype(jnp.bfloat16)
                pair = jnp.concatenate([weights.astype(jnp.bfloat16), d_scores], axis=0)
                tokens = pl.ds(pl.multiple_of(frame * per_frame, per_frame), count * per_frame)
                term = dot(pair, qd_ref[tokens, :], 1, 0)
                if fresh:
                    acc[i] = term
                else:
                    acc[i] += term
                key_rows = wide(r_ref, first + i, spaces, dim, 2 * dim)
                change = dot(key_rows, d_scores, 1, 0)
                for j in range(count):
                    d_query_ref[frame + j] += change[:, j * per_frame : (j + 1) * per_frame]

            for i in range(CLIP):
                block(i, first + i, CLIP - i, True)

            def later(queries, _):
                for i in range(CLIP):
                    block(i, queries * CLIP, CLIP, False)
                return 0

            lax.fori_loop(keys + 1, hi_ref[first] // CLIP, later, 0)
            for i in range(CLIP):
                total = acc[i]
                d_key = total[per_frame:].T[:dim]
                d_key = turned(d_key, table_ref[first + i, 0], table_ref[first + i, 1], -1.0)
                d_key = d_key.astype(jnp.bfloat16)
                d_value = total[:per_frame].T[dim:].astype(jnp.bfloat16)
                for j in range(spaces):
                    device = (first + i) * spaces + j - base
                    columns = slice(j * rows, (j + 1) * rows)
                    out[device, shift : shift + dim, :] = d_key[:, columns]
                    out[device, shift + dim : shift + 2 * dim, :] = d_value[:, columns]
            return 0

        lax.fori_loop(start, stop, group, 0)
        if last:

            def finish(frame, _):
                whole_query = d_query_ref[frame] * (1.0 / math.sqrt(dim))
                whole_query = turned(whole_query, table_ref[frame, 0], table_ref[frame, 1], -1.0)
                whole_query = whole_query.astype(jnp.bfloat16)
                for j in range(spaces):
                    out[frame * spaces + j, :dim, :] = whole_query[:, j * rows : (j + 1) * rows]
                return 0

            lax.fori_loop(0, frames, finish, 0)

    if last:
        out_shape = (devices, 3 * dim, rows)
    else:
        out_shape = ((stop - start) * CLIP * spaces, 2 * dim, rows)
    inputs = [hi, packed, d_own, lse, delta, kv, qd, tables]
    inputs += [d_query] if start else []
    inputs += list(earlier) if last else []
    return pl.pallas_call(
        body,
        out_shape=(
            jax.ShapeDtypeStruct(out_shape, jnp.bfloat16),
            jax.ShapeDtypeStruct((frames, dim, per_frame), f32),
        ),
        in_specs=[SMEM] + [VMEM] * (len(inputs) - 1),
        out_specs=(VMEM, VMEM),
        scratch_shapes=[
            pltpu.VMEM((CLIP, 2 * per_frame, 2 * dim), f32),
            pltpu.VMEM((CLIP, 2 * per_frame, 2 * dim), jnp.bfloat16),
        ],
        compiler_params=LIMIT,
        name="attend_back",
    )(*inputs)


def after(value, *others):
    return lax.optimization_barrier((value, *others))[0]


class Ring:
    def __init__(self):
        self.frames = lax.axis_size("frame")
        self.spaces = lax.axis_size("space")
        self.planes = self.frames // 4
        self.frame = lax.axis_index("frame")
        self.core = lax.axis_index("space")
        self.plane = self.frame // 4
        self.spot = self.frame % 4
        bits = (self.frame % 2, (self.frame // 2) % 2)
        self.first_bit = jnp.where(self.core == 0, bits[0], bits[1])
        self.second_bit = jnp.where(self.core == 0, bits[1], bits[0])

    def send(self, value, target):
        moves = []
        for frame in range(self.frames):
            for core in range(self.spaces):
                to_frame, to_core = target(frame, core)
                moves.append((frame * self.spaces + core, to_frame * self.spaces + to_core))
        return lax.ppermute(value, ("frame", "space"), moves)

    def first(self, value):
        return self.send(value, lambda frame, core: (frame ^ (1 if core == 0 else 2), core))

    def second(self, value):
        return self.send(value, lambda frame, core: (frame ^ (2 if core == 0 else 1), core))

    def across(self, value):
        return self.send(value, lambda frame, core: (frame, 1 - core))

    def up(self, value, step):
        size = self.frames
        return self.send(value, lambda frame, core: ((frame + 4 * step) % size, core))

    def reduce_planes(self, pieces):
        total = pieces[0].astype(jnp.float32)
        for step, piece in enumerate(pieces[1:], 1):
            total = total + self.up(piece, step).astype(jnp.float32)
        return total.astype(jnp.bfloat16)

    def spread_planes(self, value, count):
        return jnp.stack([value] + [self.up(value, step) for step in range(1, count)])

    def gather_spots(self):
        near = jnp.where(self.core == 0, 2, 1)
        own = jnp.stack([self.spot, self.spot ^ near, self.spot ^ (3 - near), self.spot ^ 3])
        other = jnp.stack([self.spot, self.spot ^ (3 - near), self.spot ^ near, self.spot ^ 3])
        cores = jnp.repeat(jnp.stack([self.core, 1 - self.core]), 4)
        return jnp.concatenate([own, other]), cores

    def gather(self, value):
        pair = jnp.stack([value, self.second(value)])
        return jnp.concatenate([pair, self.first(pair)], axis=0)

    def halve(self, value, bit, exchange):
        rows, columns = value.shape
        cut = value.reshape(2, rows // 2, columns)
        keep = lax.dynamic_index_in_dim(cut, bit, 0, keepdims=False)
        give = lax.dynamic_index_in_dim(cut, 1 - bit, 0, keepdims=False)
        return keep + exchange(give.astype(jnp.bfloat16)).astype(jnp.float32)


def quarter_rows(spots, cores):
    return jnp.where(cores == 1, spots, (spots % 2) * 2 + spots // 2)


def frame_limits(clip_frames, frames):
    ends = jnp.cumsum(clip_frames, axis=1, dtype=jnp.int32)
    begins = ends - clip_frames
    index = jnp.arange(frames, dtype=jnp.int32)[None, :, None]
    inside = (index >= begins[:, None, :]) & (index < ends[:, None, :])
    pick = lambda table: jnp.sum(jnp.where(inside, table[:, None, :], 0), axis=2, dtype=jnp.int32)
    return pick(begins), pick(ends)


def local(
    block_input,
    norm1_gain,
    w_query,
    w_key,
    w_value,
    w_out,
    norm2_gain,
    w_up,
    w_down,
    clip_frames,
    cotangent,
):
    streams, rows, width = block_input.shape
    ring = Ring()
    frames, spaces, planes = ring.frames, ring.spaces, ring.planes
    devices = frames * spaces
    per_frame = rows * spaces
    tokens = streams * rows
    axes = ("frame", "space")
    low = jnp.bfloat16
    core = jnp.reshape(ring.core, (1,))
    spots, cores = ring.gather_spots()
    slots = 4 * spaces

    owners = head_owners(frames, spaces)
    w_projections = (w_query, w_key, w_value)

    begin, end = frame_limits(clip_frames, frames)
    frame_ids = jnp.arange(frames, dtype=jnp.int32)
    mine = ring.frame * spaces + ring.core
    idle = ~jnp.any(mine == jnp.asarray(owners))
    side = ring.frame % 2
    lo = jnp.where(idle, frame_ids, jnp.where(side == 0, begin[0], begin[1]))
    hi = jnp.where(idle, frame_ids, jnp.where(side == 0, end[0], end[1]))

    def swap(value):
        return lax.all_to_all(value, axes, 0, 0, tiled=True)

    spot_of = jnp.stack([ring.frame, ring.core * rows])
    sent, normed = project(
        spot_of, clip_frames, block_input, norm1_gain, *w_projections, owners, devices, per_frame
    )
    packed = swap(sent)
    tables = rope_tables(after(lo, sent), frames, per_frame)
    neighbour = lambda value: ring.send(value, lambda frame, core: (frame ^ 1, core))
    normed_later = after(normed, packed)
    stream_near = neighbour(lax.dynamic_index_in_dim(normed_later, 1 - side, 0))
    stream_own = lax.dynamic_index_in_dim(normed_later, side, 0)
    stream_pair = jnp.where(
        side == 0,
        jnp.concatenate([stream_own, stream_near]),
        jnp.concatenate([stream_near, stream_own]),
    )
    same_side = [list(range(start, frames, 2)) for start in range(2)]
    stream_mine = lax.all_gather(
        stream_pair, "frame", axis=0, tiled=True, axis_index_groups=same_side
    )
    cot_flat = cotangent.reshape(tokens, width)
    cot_one = ring.second(after(cot_flat, packed))
    out, out_low, lse, kv = attend(lo, packed, frames)
    attended = swap(out_low)
    cot_pair = after(jnp.stack([cot_flat, cot_one]), out_low)
    cot_mine = jnp.concatenate([cot_pair, ring.first(cot_pair)], axis=0)

    middle, two = attention_out(attended, block_input, w_out, norm2_gain, owners)
    cot_other = ring.across(after(cot_mine, middle))
    chunk, skip = 512, 3
    so_far = feed_first(two, cotangent, w_up, w_down, chunk, skip)
    two_pair = jnp.stack([two, ring.second(two)])
    so_far = after(so_far, two_pair)
    two_mine = jnp.concatenate([two_pair, ring.first(two_pair)], axis=0)
    block_output, d_middle, d_sent, out_keep, out_give = feed_rest(
        core, so_far, attended, middle, two, cotangent, w_out, norm2_gain, w_up, w_down,
        chunk, skip, owners,
    )
    d_own = swap(d_sent)
    two_other = ring.across(two_mine)
    out_sum = out_keep + ring.across(out_give).astype(jnp.float32)
    out_sum = ring.halve(out_sum, ring.first_bit, ring.first)
    out_sum = ring.halve(out_sum, ring.second_bit, ring.second)
    pieces = hidden_gradients(
        jnp.stack([ring.spot * spaces + ring.core, ring.plane]),
        two_mine, two_other, cot_mine, cot_other, w_up, w_down, out_sum, slots, planes,
    )

    total = ring.reduce_planes(pieces)
    stream_other = ring.across(stream_mine)
    qd, delta = attend_back_ready(packed, after(d_own, pieces[0]), out, frames)
    groups = frames // CLIP
    cuts = [0, groups // 4, groups // 2, groups]
    d_query, earlier = None, []
    for start, stop in zip(cuts[:-1], cuts[1:]):
        delta_now = after(delta, total) if stop == groups else delta
        result, d_query = attend_back(
            hi, packed, d_own, lse, delta_now, kv, qd, tables, d_query, earlier, frames, start, stop
        )
        earlier.append(result)
    hidden_mine = ring.gather(ring.spread_planes(total, planes))
    back = swap(result)
    hidden_other = ring.across(hidden_mine)
    unit_slots = spots * spaces + cores
    where = jnp.stack(
        [unit_slots, quarter_rows(spots, cores), cores, jnp.broadcast_to(ring.plane, cores.shape)]
    )
    grad_up, grad_down, grad_out, gain_two = place_hidden(
        where, hidden_mine, hidden_other, w_up, w_out, norm2_gain, slots
    )

    keep, give = head_products(jnp.stack([ring.core, side]), result, stream_mine, stream_other)
    heads_sum = (keep + neighbour(give).astype(jnp.float32)).astype(low)
    heads_mine = ring.gather(ring.spread_planes(heads_sum, planes))
    heads_other = ring.across(heads_mine)
    owner_of = jnp.asarray([[owners[stream][head] for head in range(HEADS)] for stream in range(2)])
    owner_plane, owner_spot = owner_of // (4 * spaces), owner_of // spaces % 4
    owner_core = owner_of % spaces
    list_of = jnp.where(owner_core == ring.core, 0, 1)
    entries = jnp.stack([spots[:4], spots[4:]])[list_of] == owner_spot[..., None]
    entry = jnp.sum(jnp.where(entries, jnp.arange(4), 0), axis=-1)
    entry = entry * planes + (ring.plane - owner_plane) % planes
    where = jnp.concatenate([entry, jnp.broadcast_to(ring.core, (1, HEADS))]).astype(jnp.int32)
    flat = lambda value: value.reshape((-1,) + value.shape[2:])
    grad_query, grad_key, grad_value, gain_one = place_heads(
        where, flat(heads_mine), flat(heads_other), w_projections, norm1_gain, owners
    )
    grad_input = input_gradient(back, w_projections, block_input, norm1_gain, d_middle, owners)
    return (
        block_output,
        grad_input,
        gain_one.reshape(width),
        grad_query,
        grad_key,
        grad_value,
        grad_out,
        gain_two.reshape(width),
        grad_up,
        grad_down,
    )


def solution(mesh):
    spread = P(None, ("frame", "space"), None)
    in_specs = (spread,) + (P(),) * 9 + (spread,)
    out_specs = (spread, spread) + (P(),) * 8
    return jax.shard_map(local, mesh=mesh, in_specs=in_specs, out_specs=out_specs, check_vma=False)
```

profile of v0, /device:TPU:0, one launch (start us, length us, event | category | flops | bytes accessed | tf_op | source)
XLA Modules:
  0.0 473.0 jit_solution(13686634969413817787)
XLA Ops:
  13.7 7.3 %all-to-all-start = ((bf16[32,192,128]{2,1,0:T(8,128)(2,1)}), bf16[32,192,128]{2,1,0:T(8,128)(2,1)S(1)}, u32[]{:S(2)}, u32[]{:S(2)}) async-start(bf16[32,192,128]{2,1,0:T(8,128)(2,1)} %get-tuple-element.55), calls=%async_computation | async-start | bytes 3145728 | tf_op jit(solution)/shard_map/all_to_all | solution.py:923
  23.2 35.5 %all-to-all-done.r_ref = bf16[32,192,128]{2,1,0:T(8,128)(2,1)S(1)} async-done(((bf16[32,192,128]{2,1,0:T(8,128)(2,1)}), bf16[32,192,128]{2,1,0:T(8,128)(2,1)S(1)}, u32[]{:S(2)}, u32[]{:S(2)}) %all-to-all-start) | async-done | bytes 1572896 | tf_op jit(solution)/shard_map/all_to_all | solution.py:923
  59.9 28.7 %attend.1 = (f32[32,64,128]{2,1,0:T(8,128)}, bf16[32,64,128]{2,1,0:T(8,128)(2,1)}, f32[16,1,256]{2,1,0:T(1,128)}, bf16[4096,128]{1,0:T(8,128)(2,1)}) custom-call(s32[16]{0:T(128)} %broadcast_select_fusion.3.lo_ref, bf16[32,192,128]{2,1,0:T(8,128)(2,1)} %copy-done), custom_call_target="tpu_custom_call" | custom-call | tf_op jit(solution)/shard_map/attend/pallas_call | solution.py:638
  95.4 11.4 %all-to-all-done.1.att = bf16[32,64,128]{2,1,0:T(8,128)(2,1)S(1)} async-done(((bf16[32,64,128]{2,1,0:T(8,128)(2,1)}), bf16[32,64,128]{2,1,0:T(8,128)(2,1)S(1)}, u32[]{:S(2)}, u32[]{:S(2)}) %all-to-all-start.1) | async-done | bytes 524320 | tf_op jit(solution)/shard_map/all_to_all | solution.py:923
  114.1 9.4 %collective-permute-done = bf16[256,768]{1,0:T(8,128)(2,1)S(1)} collective-permute-done((bf16[256,768]{1,0:T(8,128)(2,1)}, bf16[256,768]{1,0:T(8,128)(2,1)S(1)}, u32[]{:S(2)}, u32[]{:S(2)}) %collective-permute-start) | collective-permute-done | bytes 393248 | tf_op jit(solution)/shard_map/ppermute | solution.py:830
  124.9 6.6 %feed_first.1 = (f32[256,768]{1,0:T(8,128)}, f32[256,768]{1,0:T(8,128)}) custom-call(bf16[256,768]{1,0:T(8,128)(2,1)} %get-tuple-element.57.two_ref, bf16[2,128,768]{2,1,0:T(8,128)(2,1)} %cot.3, bf16[768,3072]{1,0:T(8,128)(2,1)} %up_ref.1, bf16[3072,768]{1,0:T(8,128)(2,1)} %down.5), custom_call_target="tpu_custom_call" | custom-call | tf_op jit(solution)/shard_map/feed_first/pallas_call | solution.py:209
  131.5 10.2 %feed_rest.1 = (bf16[2,128,768]{2,1,0:T(8,128)(2,1)}, f32[256,768]{1,0:T(8,128)}, bf16[32,64,128]{2,1,0:T(8,128)(2,1)}, f32[768,384]{1,0:T(8,128)}, bf16[768,384]{1,0:T(8,128)(2,1)}) custom-call(s32[1]{0:T(128)} %bitcast.core_ref, f32[256,768]{1,0:T(8,128)} %get-tuple-element.60.first_result, f32[256,768]{1,0:T(8,128)} %get-tuple-element.61.first_two, ...), custom_call_target="tpu_custom_call" | custom-call | tf_op jit(solution)/shard_map/feed_rest/pallas_call | solution.py:287
  147.8 6.1 %collective-permute-done.7 = bf16[384,384]{1,0:T(8,128)(2,1)} collective-permute-done((bf16[384,384]{1,0:T(8,128)(2,1)S(1)}, bf16[384,384]{1,0:T(8,128)(2,1)}, u32[]{:S(2)}, u32[]{:S(2)}) %collective-permute-start.7) | collective-permute-done | bytes 294944 | tf_op jit(solution)/shard_map/ppermute | solution.py:830
  158.0 6.0 %collective-permute-done.8 = bf16[192,384]{1,0:T(8,128)(2,1)S(1)} collective-permute-done((bf16[192,384]{1,0:T(8,128)(2,1)S(1)}, bf16[192,384]{1,0:T(8,128)(2,1)S(1)}, u32[]{:S(2)}, u32[]{:S(2)}) %collective-permute-start.8) | collective-permute-done | bytes 147488 | tf_op jit(solution)/shard_map/ppermute | solution.py:830
  164.7 12.4 %hidden_gradients.1 = (bf16[432,384]{1,0:T(8,128)(2,1)}, bf16[432,384]{1,0:T(8,128)(2,1)}, bf16[432,384]{1,0:T(8,128)(2,1)}, bf16[432,384]{1,0:T(8,128)(2,1)}) custom-call(s32[2]{0:T(128)} %pad_add_fusion.2.where_ref, bf16[4,256,768]{2,1,0:T(8,128)(2,1)} %copy-done.5, bf16[4,256,768]{2,1,0:T(8,128)(2,1)} %collective-permute-done.2.two_b, ...), custom_call_target="tpu_custom_call" | custom-call | tf_op jit(solution)/shard_map/hidden_gradients/pallas_call | solution.py:367
  179.3 16.9 %collective-permute-done.10 = bf16[432,384]{1,0:T(8,128)(2,1)S(1)} collective-permute-done((bf16[432,384]{1,0:T(8,128)(2,1)}, bf16[432,384]{1,0:T(8,128)(2,1)S(1)}, u32[]{:S(2)}, u32[]{:S(2)}) %collective-permute-start.10) | collective-permute-done | bytes 331808 | tf_op jit(solution)/shard_map/ppermute | solution.py:830
  196.1 5.0 %collective-permute-done.9 = bf16[432,384]{1,0:T(8,128)(2,1)S(1)} collective-permute-done((bf16[432,384]{1,0:T(8,128)(2,1)}, bf16[432,384]{1,0:T(8,128)(2,1)S(1)}, u32[]{:S(2)}, u32[]{:S(2)}) %collective-permute-start.9) | collective-permute-done | bytes 331808 | tf_op jit(solution)/shard_map/ppermute | solution.py:830
  202.3 15.8 %collective-permute-start.21 = (bf16[432,384]{1,0:T(8,128)(2,1)S(1)}, bf16[432,384]{1,0:T(8,128)(2,1)S(1)}, u32[]{:S(2)}, u32[]{:S(2)}) collective-permute-start(bf16[432,384]{1,0:T(8,128)(2,1)S(1)} %add_convert_fusion), channel_id=1, source_target_pairs={{0,8},{1,9},{2,10},{3,11},{4,12},{5,13},{6,14},{7,15},{8,16},{9,17... | collective-permute-start | bytes 995336 | tf_op jit(solution)/shard_map/ppermute | solution.py:830
  220.7 5.5 %collective-permute-done.21 = bf16[432,384]{1,0:T(8,128)(2,1)S(1)} collective-permute-done((bf16[432,384]{1,0:T(8,128)(2,1)S(1)}, bf16[432,384]{1,0:T(8,128)(2,1)S(1)}, u32[]{:S(2)}, u32[]{:S(2)}) %collective-permute-start.21) | collective-permute-done | bytes 331808 | tf_op jit(solution)/shard_map/ppermute | solution.py:830
  226.2 9.3 %collective-permute-done.22 = bf16[432,384]{1,0:T(8,128)(2,1)S(1)} collective-permute-done((bf16[432,384]{1,0:T(8,128)(2,1)S(1)}, bf16[432,384]{1,0:T(8,128)(2,1)S(1)}, u32[]{:S(2)}, u32[]{:S(2)}) %collective-permute-start.22) | collective-permute-done | bytes 331808 | tf_op jit(solution)/shard_map/ppermute | solution.py:830
  241.8 16.0 %collective-permute-done.24 = bf16[4,432,384]{2,1,0:T(8,128)(2,1)S(1)} collective-permute-done((bf16[4,432,384]{2,1,0:T(8,128)(2,1)S(1)}, bf16[4,432,384]{2,1,0:T(8,128)(2,1)S(1)}, u32[]{:S(2)}, u32[]{:S(2)}) %collective-permute-start.24) | collective-permute-done | bytes 1327136 | tf_op jit(solution)/shard_map/ppermute | solution.py:830
  261.2 11.7 %all-to-all-start.2 = ((bf16[32,64,128]{2,1,0:T(8,128)(2,1)}), bf16[32,64,128]{2,1,0:T(8,128)(2,1)S(1)}, u32[]{:S(2)}, u32[]{:S(2)}) async-start(bf16[32,64,128]{2,1,0:T(8,128)(2,1)} %get-tuple-element.64), calls=%async_computation.2 | async-start | bytes 1048576 | tf_op jit(solution)/shard_map/all_to_all | solution.py:923
  277.5 19.3 %collective-permute-done.25 = bf16[2,4,432,384]{3,2,1,0:T(8,128)(2,1)} collective-permute-done((bf16[2,4,432,384]{3,2,1,0:T(8,128)(2,1)}, bf16[2,4,432,384]{3,2,1,0:T(8,128)(2,1)}, u32[]{:S(2)}, u32[]{:S(2)}) %collective-permute-start.25) | collective-permute-done | bytes 2654240 | tf_op jit(solution)/shard_map/ppermute | solution.py:830
  306.5 13.5 %attend_back.3 = (bf16[8,128,128]{2,1,0:T(8,128)(2,1)}, f32[16,64,256]{2,1,0:T(8,128)}) custom-call(s32[16]{0:T(128)} %broadcast_select_fusion.2.hi_ref, bf16[32,192,128]{2,1,0:T(8,128)(2,1)} %copy-done, bf16[32,64,128]{2,1,0:T(8,128)(2,1)} %copy-done.1, f32[16,1,256]{2,1,0:T(1,128)} %get-tuple-element.65.lse_ref, ...), custom_call_target="tpu_custom_call" | custom-call | tf_op jit(solution)/shard_map/attend_back/pallas_call | solution.py:790
  320.0 11.5 %attend_back.4 = (bf16[8,128,128]{2,1,0:T(8,128)(2,1)}, f32[16,64,256]{2,1,0:T(8,128)}) custom-call(s32[16]{0:T(128)} %broadcast_select_fusion.2.hi_ref, bf16[32,192,128]{2,1,0:T(8,128)(2,1)} %copy-done, bf16[32,64,128]{2,1,0:T(8,128)(2,1)} %copy-done.1, f32[16,1,256]{2,1,0:T(1,128)} %get-tuple-element.65.lse_ref, ...), custom_call_target="tpu_custom_call" | custom-call | tf_op jit(solution)/shard_map/attend_back/pallas_call | solution.py:790
  331.5 11.7 %attend_back.5 = (bf16[32,192,128]{2,1,0:T(8,128)(2,1)}, f32[16,64,256]{2,1,0:T(8,128)}) custom-call(s32[16]{0:T(128)} %broadcast_select_fusion.2.hi_ref, bf16[32,192,128]{2,1,0:T(8,128)(2,1)} %copy-done, bf16[32,64,128]{2,1,0:T(8,128)(2,1)} %copy-done.1, f32[16,1,256]{2,1,0:T(1,128)} %get-tuple-element.65.lse_ref, ...), custom_call_target="tpu_custom_call" | custom-call | tf_op jit(solution)/shard_map/attend_back/pallas_call | solution.py:790
  343.2 6.8 %head_products.1 = (f32[192,384]{1,0:T(8,128)}, bf16[192,384]{1,0:T(8,128)(2,1)}) custom-call(s32[2]{0:T(128)} %pad_add_fusion.3.where_ref, bf16[32,192,128]{2,1,0:T(8,128)(2,1)} %get-tuple-element.86.d_ref, bf16[16,128,768]{2,1,0:T(8,128)(2,1)} %all-gather.2.cloned.1.call-done.a_ref, bf16[16,128,768]{2,1,0:T(8,128)(2,1)} %collective-permute-done.13.b_ref), custom_call_target="tpu_custom_call" | custom-call | tf_op jit(solution)/shard_map/head_products/pallas_call | solution.py:504
  350.0 6.5 %collective-permute-done.14 = bf16[192,384]{1,0:T(8,128)(2,1)S(1)} collective-permute-done((bf16[192,384]{1,0:T(8,128)(2,1)}, bf16[192,384]{1,0:T(8,128)(2,1)S(1)}, u32[]{:S(2)}, u32[]{:S(2)}) %collective-permute-start.14) | collective-permute-done | bytes 147488 | tf_op jit(solution)/shard_map/ppermute | solution.py:830
  357.5 7.4 %collective-permute-start.15 = (bf16[192,384]{1,0:T(8,128)(2,1)S(1)}, bf16[192,384]{1,0:T(8,128)(2,1)S(1)}, u32[]{:S(2)}, u32[]{:S(2)}) collective-permute-start(bf16[192,384]{1,0:T(8,128)(2,1)S(1)} %add_convert_fusion.1), channel_id=1, source_target_pairs={{0,8},{1,9},{2,10},{3,11},{4,12},{5,13},{6,14},{7,15},{8,16},{9,17... | collective-permute-start | bytes 442376 | tf_op jit(solution)/shard_map/ppermute | solution.py:830
  372.5 5.4 %collective-permute-done.16 = bf16[192,384]{1,0:T(8,128)(2,1)S(1)} collective-permute-done((bf16[192,384]{1,0:T(8,128)(2,1)S(1)}, bf16[192,384]{1,0:T(8,128)(2,1)S(1)}, u32[]{:S(2)}, u32[]{:S(2)}) %collective-permute-start.16) | collective-permute-done | bytes 147488 | tf_op jit(solution)/shard_map/ppermute | solution.py:830
  378.1 9.9 %collective-permute-done.18 = bf16[4,192,384]{2,1,0:T(8,128)(2,1)S(1)} collective-permute-done((bf16[4,192,384]{2,1,0:T(8,128)(2,1)S(1)}, bf16[4,192,384]{2,1,0:T(8,128)(2,1)S(1)}, u32[]{:S(2)}, u32[]{:S(2)}) %collective-permute-start.18) | collective-permute-done | bytes 589856 | tf_op jit(solution)/shard_map/ppermute | solution.py:830
  388.6 5.1 %all-to-all-start.3 = ((bf16[32,192,128]{2,1,0:T(8,128)(2,1)}), bf16[32,192,128]{2,1,0:T(8,128)(2,1)}, u32[]{:S(2)}, u32[]{:S(2)}) async-start(bf16[32,192,128]{2,1,0:T(8,128)(2,1)} %get-tuple-element.86.d_ref), calls=%async_computation.3 | async-start | bytes 3145728 | tf_op jit(solution)/shard_map/all_to_all | solution.py:923
  393.8 22.3 %collective-permute-done.19 = bf16[2,4,192,384]{3,2,1,0:T(8,128)(2,1)} collective-permute-done((bf16[2,4,192,384]{3,2,1,0:T(8,128)(2,1)S(1)}, bf16[2,4,192,384]{3,2,1,0:T(8,128)(2,1)}, u32[]{:S(2)}, u32[]{:S(2)}) %collective-permute-start.19) | collective-permute-done | bytes 1179680 | tf_op jit(solution)/shard_map/ppermute | solution.py:830
  423.1 8.4 %all-to-all-done.3.d_ref = bf16[32,192,128]{2,1,0:T(8,128)(2,1)} async-done(((bf16[32,192,128]{2,1,0:T(8,128)(2,1)}), bf16[32,192,128]{2,1,0:T(8,128)(2,1)}, u32[]{:S(2)}, u32[]{:S(2)}) %all-to-all-start.3) | async-done | bytes 1572896 | tf_op jit(solution)/shard_map/all_to_all | solution.py:923
  431.6 6.3 %input_gradient.1 = f32[2,128,768]{2,1,0:T(8,128)} custom-call(bf16[32,192,128]{2,1,0:T(8,128)(2,1)} %all-to-all-done.3.d_ref, bf16[768,768]{1,0:T(8,128)(2,1)} %wq.5, bf16[768,768]{1,0:T(8,128)(2,1)} %wk.5, bf16[768,768]{1,0:T(8,128)(2,1)} %wv.5, bf16[2,128,768]{2,1,0:T(8,128)(2,1)} %x_ref.5, f32[1,768]{1,0:T(1,128)} %broadcast_in_dim.54.gain_ref, ...), custom_call_target="tpu_custom_call" | custom-call | tf_op jit(solution)/shard_map/input_gradient/pallas_call | solution.py:565
  437.9 7.4 %place_heads.1 = (f32[768,768]{1,0:T(8,128)}, f32[768,768]{1,0:T(8,128)}, f32[768,768]{1,0:T(8,128)}, f32[768,1]{1,0:T(8,128)}) custom-call(s32[3,12]{1,0:T(4,128)} %concatenate.82.where_ref, bf16[16,192,384]{2,1,0:T(8,128)(2,1)} %bitcast.61, bf16[16,192,384]{2,1,0:T(8,128)(2,1)} %bitcast.32.other_ref, bf16[768,768]{1,0:T(8,128)(2,1)} %wq.5, ...), custom_call_target="tpu_custom_call" | custom-call | tf_op jit(solution)/shard_map/place_heads/pallas_call | solution.py:540
  447.1 16.9 %place_hidden.1 = (f32[768,3072]{1,0:T(8,128)}, f32[3072,768]{1,0:T(8,128)}, f32[768,768]{1,0:T(8,128)}, f32[768,1]{1,0:T(8,128)}) custom-call(s32[4,8]{1,0:T(4,128)} %add_add_fusion.where_ref, bf16[4,4,432,384]{3,2,1,0:T(8,128)(2,1)} %pad_maximum_fusion.mine_ref, bf16[4,4,432,384]{3,2,1,0:T(8,128)(2,1)} %collective-permute-done.26.other_ref, ...), custom_call_target="tpu_custom_call" | custom-call | tf_op jit(solution)/shard_map/place_hidden/pallas_call | solution.py:444
  (133 shorter events, 85.3 us)
Async XLA Ops:
  13.7 45.0 %all-to-all-start = ((bf16[32,192,128]{2,1,0:T(8,128)(2,1)}), bf16[32,192,128]{2,1,0:T(8,128)(2,1)S(1)}, u32[]{:S(2)}, u32[]{:S(2)}) async-start(bf16[32,192,128]{2,1,0:T(8,128)(2,1)} %get-tuple-element.55), calls=%async_computation | async-start | bytes 3145728 | tf_op jit(solution)/shard_map/all_to_all | solution.py:923
  88.6 18.2 %all-to-all-start.1 = ((bf16[32,64,128]{2,1,0:T(8,128)(2,1)}), bf16[32,64,128]{2,1,0:T(8,128)(2,1)S(1)}, u32[]{:S(2)}, u32[]{:S(2)}) async-start(bf16[32,64,128]{2,1,0:T(8,128)(2,1)} %get-tuple-element.56), calls=%async_computation.1 | async-start | bytes 1048576 | tf_op jit(solution)/shard_map/all_to_all | solution.py:923
  91.3 170.0 %all-gather.2.cloned.1.call-start = ((), (), s32[]{:S(2)}) async-start(), calls=%async_computation.4 | async-start | bytes 3538944 | tf_op jit(solution)/shard_map/all_gather | solution.py:941
  91.5 21.3 %collective-permute-start.3 = (bf16[256,768]{1,0:T(8,128)(2,1)S(1)}, bf16[256,768]{1,0:T(8,128)(2,1)S(1)}, u32[]{:S(2)}, u32[]{:S(2)}) collective-permute-start(bf16[256,768]{1,0:T(8,128)(2,1)S(1)} %bitcast.68), channel_id=1, source_target_pairs={{0,4},{1,3},{2,6},{3,1},{4,0},{5,7},{6,2},{7,5},{8,12},{9,11},{10,... | collective-permute-start | bytes 1179656 | tf_op jit(solution)/shard_map/ppermute | solution.py:830
  93.2 18.7 %collective-permute-start.12 = (bf16[1,128,768]{2,1,0:T(8,128)(2,1)S(1)}, bf16[1,128,768]{2,1,0:T(8,128)(2,1)S(1)}, u32[]{:S(2)}, u32[]{:S(2)}) collective-permute-start(bf16[1,128,768]{2,1,0:T(8,128)(2,1)S(1)} %get-tuple-element.107), channel_id=1, source_target_pairs={{0,2},{1,3},{2,0},{3,1},{4,6},{5,7},{6,4},{7,5},{8,10},{9,11},{10,... | collective-permute-start | bytes 589832 | tf_op jit(solution)/shard_map/ppermute | solution.py:830
  110.7 12.7 %collective-permute-start = (bf16[256,768]{1,0:T(8,128)(2,1)}, bf16[256,768]{1,0:T(8,128)(2,1)S(1)}, u32[]{:S(2)}, u32[]{:S(2)}) collective-permute-start(bf16[256,768]{1,0:T(8,128)(2,1)} %get-tuple-element.57.two_ref), channel_id=1, source_target_pairs={{0,4},{1,3},{2,6},{3,1},{4,0},{5,7},{6,2},{7,5},{8,12},{9,11},{10,... | collective-permute-start | bytes 1179656 | tf_op jit(solution)/shard_map/ppermute | solution.py:830
  112.9 29.8 %collective-permute-start.4 = (bf16[2,256,768]{2,1,0:T(8,128)(2,1)S(1)}, bf16[2,256,768]{2,1,0:T(8,128)(2,1)S(1)}, u32[]{:S(2)}, u32[]{:S(2)}) collective-permute-start(bf16[2,256,768]{2,1,0:T(8,128)(2,1)S(1)} %pad_maximum_fusion.7), channel_id=1, source_target_pairs={{0,2},{1,5},{2,0},{3,7},{4,6},{5,1},{6,4},{7,3},{8,10},{9,13},{10,... | collective-permute-start | bytes 2359304 | tf_op jit(solution)/shard_map/ppermute | solution.py:830
  123.6 20.6 %collective-permute-start.1 = (bf16[2,256,768]{2,1,0:T(8,128)(2,1)S(1)}, bf16[2,256,768]{2,1,0:T(8,128)(2,1)S(1)}, u32[]{:S(2)}, u32[]{:S(2)}) collective-permute-start(bf16[2,256,768]{2,1,0:T(8,128)(2,1)S(1)} %pad_maximum_fusion.6), channel_id=1, source_target_pairs={{0,2},{1,5},{2,0},{3,7},{4,6},{5,1},{6,4},{7,3},{8,10},{9,13},{10,... | collective-permute-start | bytes 2359304 | tf_op jit(solution)/shard_map/ppermute | solution.py:830
  141.7 2.7 collective-permute-start.6
  143.6 21.1 %collective-permute-start.5 = (bf16[4,256,768]{2,1,0:T(8,128)(2,1)}, bf16[4,256,768]{2,1,0:T(8,128)(2,1)}, u32[]{:S(2)}, u32[]{:S(2)}) collective-permute-start(bf16[4,256,768]{2,1,0:T(8,128)(2,1)} %constant_dynamic-update-slice_fusion.cot_a), channel_id=1, source_target_pairs={{0,1},{1,0},{2,3},{3,2},{4,5},{5,4},{6,7},{7,6},{8,9},{9,8},{10,11... | collective-permute-start | bytes 4718600 | tf_op jit(solution)/shard_map/ppermute | solution.py:830
  144.3 20.5 %collective-permute-start.2 = (bf16[4,256,768]{2,1,0:T(8,128)(2,1)S(1)}, bf16[4,256,768]{2,1,0:T(8,128)(2,1)}, u32[]{:S(2)}, u32[]{:S(2)}) collective-permute-start(bf16[4,256,768]{2,1,0:T(8,128)(2,1)S(1)} %pad_maximum_fusion.3.two_a), channel_id=1, source_target_pairs={{0,1},{1,0},{2,3},{3,2},{4,5},{5,4},{6,7},{7,6},{8,9},{9,8},{10,11... | collective-permute-start | bytes 4718600 | tf_op jit(solution)/shard_map/ppermute | solution.py:830
  147.0 6.9 %collective-permute-start.7 = (bf16[384,384]{1,0:T(8,128)(2,1)S(1)}, bf16[384,384]{1,0:T(8,128)(2,1)}, u32[]{:S(2)}, u32[]{:S(2)}) collective-permute-start(bf16[384,384]{1,0:T(8,128)(2,1)S(1)} %fusion), channel_id=1, source_target_pairs={{0,2},{1,5},{2,0},{3,7},{4,6},{5,1},{6,4},{7,3},{8,10},{9,13},{10,... | collective-permute-start | bytes 884744 | tf_op jit(solution)/shard_map/ppermute | solution.py:830
  154.9 9.1 %collective-permute-start.8 = (bf16[192,384]{1,0:T(8,128)(2,1)S(1)}, bf16[192,384]{1,0:T(8,128)(2,1)S(1)}, u32[]{:S(2)}, u32[]{:S(2)}) collective-permute-start(bf16[192,384]{1,0:T(8,128)(2,1)S(1)} %fusion.1), channel_id=1, source_target_pairs={{0,4},{1,3},{2,6},{3,1},{4,0},{5,7},{6,2},{7,5},{8,12},{9,11},{10,... | collective-permute-start | bytes 442376 | tf_op jit(solution)/shard_map/ppermute | solution.py:830
  177.2 18.9 %collective-permute-start.10 = (bf16[432,384]{1,0:T(8,128)(2,1)}, bf16[432,384]{1,0:T(8,128)(2,1)S(1)}, u32[]{:S(2)}, u32[]{:S(2)}) collective-permute-start(bf16[432,384]{1,0:T(8,128)(2,1)} %get-tuple-element.76), channel_id=1, source_target_pairs={{0,16},{1,17},{2,18},{3,19},{4,20},{5,21},{6,22},{7,23},{8,24},{9,... | collective-permute-start | bytes 995336 | tf_op jit(solution)/shard_map/ppermute | solution.py:830
  177.2 18.9 %collective-permute-start.11 = (bf16[432,384]{1,0:T(8,128)(2,1)}, bf16[432,384]{1,0:T(8,128)(2,1)S(1)}, u32[]{:S(2)}, u32[]{:S(2)}) collective-permute-start(bf16[432,384]{1,0:T(8,128)(2,1)} %get-tuple-element.77), channel_id=1, source_target_pairs={{0,24},{1,25},{2,26},{3,27},{4,28},{5,29},{6,30},{7,31},{8,0},{9,1... | collective-permute-start | bytes 995336 | tf_op jit(solution)/shard_map/ppermute | solution.py:830
  179.0 22.1 %collective-permute-start.9 = (bf16[432,384]{1,0:T(8,128)(2,1)}, bf16[432,384]{1,0:T(8,128)(2,1)S(1)}, u32[]{:S(2)}, u32[]{:S(2)}) collective-permute-start(bf16[432,384]{1,0:T(8,128)(2,1)} %get-tuple-element.75), channel_id=1, source_target_pairs={{0,8},{1,9},{2,10},{3,11},{4,12},{5,13},{6,14},{7,15},{8,16},{9,17... | collective-permute-start | bytes 995336 | tf_op jit(solution)/shard_map/ppermute | solution.py:830
  202.3 24.0 %collective-permute-start.21 = (bf16[432,384]{1,0:T(8,128)(2,1)S(1)}, bf16[432,384]{1,0:T(8,128)(2,1)S(1)}, u32[]{:S(2)}, u32[]{:S(2)}) collective-permute-start(bf16[432,384]{1,0:T(8,128)(2,1)S(1)} %add_convert_fusion), channel_id=1, source_target_pairs={{0,8},{1,9},{2,10},{3,11},{4,12},{5,13},{6,14},{7,15},{8,16},{9,17... | collective-permute-start | bytes 995336 | tf_op jit(solution)/shard_map/ppermute | solution.py:830
  218.1 17.4 %collective-permute-start.22 = (bf16[432,384]{1,0:T(8,128)(2,1)S(1)}, bf16[432,384]{1,0:T(8,128)(2,1)S(1)}, u32[]{:S(2)}, u32[]{:S(2)}) collective-permute-start(bf16[432,384]{1,0:T(8,128)(2,1)S(1)} %add_convert_fusion), channel_id=1, source_target_pairs={{0,16},{1,17},{2,18},{3,19},{4,20},{5,21},{6,22},{7,23},{8,24},{9,... | collective-permute-start | bytes 995336 | tf_op jit(solution)/shard_map/ppermute | solution.py:830
  218.1 21.6 %collective-permute-start.23 = (bf16[432,384]{1,0:T(8,128)(2,1)S(1)}, bf16[432,384]{1,0:T(8,128)(2,1)S(1)}, u32[]{:S(2)}, u32[]{:S(2)}) collective-permute-start(bf16[432,384]{1,0:T(8,128)(2,1)S(1)} %add_convert_fusion), channel_id=1, source_target_pairs={{0,24},{1,25},{2,26},{3,27},{4,28},{5,29},{6,30},{7,31},{8,0},{9,1... | collective-permute-start | bytes 995336 | tf_op jit(solution)/shard_map/ppermute | solution.py:830
  239.9 17.8 %collective-permute-start.24 = (bf16[4,432,384]{2,1,0:T(8,128)(2,1)S(1)}, bf16[4,432,384]{2,1,0:T(8,128)(2,1)S(1)}, u32[]{:S(2)}, u32[]{:S(2)}) collective-permute-start(bf16[4,432,384]{2,1,0:T(8,128)(2,1)S(1)} %get-tuple-element.103), channel_id=1, source_target_pairs={{0,4},{1,3},{2,6},{3,1},{4,0},{5,7},{6,2},{7,5},{8,12},{9,11},{10,... | collective-permute-start | bytes 3981320 | tf_op jit(solution)/shard_map/ppermute | solution.py:830
  259.6 37.2 %collective-permute-start.25 = (bf16[2,4,432,384]{3,2,1,0:T(8,128)(2,1)}, bf16[2,4,432,384]{3,2,1,0:T(8,128)(2,1)}, u32[]{:S(2)}, u32[]{:S(2)}) collective-permute-start(bf16[2,4,432,384]{3,2,1,0:T(8,128)(2,1)} %pad_maximum_fusion.1), channel_id=1, source_target_pairs={{0,2},{1,5},{2,0},{3,7},{4,6},{5,1},{6,4},{7,3},{8,10},{9,13},{10,... | collective-permute-start | bytes 7962632 | tf_op jit(solution)/shard_map/ppermute | solution.py:830
  261.2 82.0 %collective-permute-start.13 = (bf16[16,128,768]{2,1,0:T(8,128)(2,1)}, bf16[16,128,768]{2,1,0:T(8,128)(2,1)}, u32[]{:S(2)}, u32[]{:S(2)}) collective-permute-start(bf16[16,128,768]{2,1,0:T(8,128)(2,1)} %all-gather.2.cloned.1.call-done.a_ref), channel_id=1, source_target_pairs={{0,1},{1,0},{2,3},{3,2},{4,5},{5,4},{6,7},{7,6},{8,9},{9,8},{10,11... | collective-permute-start | bytes 9437192 | tf_op jit(solution)/shard_map/ppermute | solution.py:830
  261.2 40.8 %all-to-all-start.2 = ((bf16[32,64,128]{2,1,0:T(8,128)(2,1)}), bf16[32,64,128]{2,1,0:T(8,128)(2,1)S(1)}, u32[]{:S(2)}, u32[]{:S(2)}) async-start(bf16[32,64,128]{2,1,0:T(8,128)(2,1)} %get-tuple-element.64), calls=%async_computation.2 | async-start | bytes 1048576 | tf_op jit(solution)/shard_map/all_to_all | solution.py:923
  301.6 145.5 %collective-permute-start.26 = (bf16[4,4,432,384]{3,2,1,0:T(8,128)(2,1)}, bf16[4,4,432,384]{3,2,1,0:T(8,128)(2,1)}, u32[]{:S(2)}, u32[]{:S(2)}) collective-permute-start(bf16[4,4,432,384]{3,2,1,0:T(8,128)(2,1)} %pad_maximum_fusion.mine_ref), channel_id=1, source_target_pairs={{0,1},{1,0},{2,3},{3,2},{4,5},{5,4},{6,7},{7,6},{8,9},{9,8},{10,11... | collective-permute-start | bytes 15925256 | tf_op jit(solution)/shard_map/ppermute | solution.py:830
  350.0 6.5 %collective-permute-start.14 = (bf16[192,384]{1,0:T(8,128)(2,1)}, bf16[192,384]{1,0:T(8,128)(2,1)S(1)}, u32[]{:S(2)}, u32[]{:S(2)}) collective-permute-start(bf16[192,384]{1,0:T(8,128)(2,1)} %get-tuple-element.91), channel_id=1, source_target_pairs={{0,2},{1,3},{2,0},{3,1},{4,6},{5,7},{6,4},{7,5},{8,10},{9,11},{10,... | collective-permute-start | bytes 442376 | tf_op jit(solution)/shard_map/ppermute | solution.py:830
  357.5 15.0 %collective-permute-start.15 = (bf16[192,384]{1,0:T(8,128)(2,1)S(1)}, bf16[192,384]{1,0:T(8,128)(2,1)S(1)}, u32[]{:S(2)}, u32[]{:S(2)}) collective-permute-start(bf16[192,384]{1,0:T(8,128)(2,1)S(1)} %add_convert_fusion.1), channel_id=1, source_target_pairs={{0,8},{1,9},{2,10},{3,11},{4,12},{5,13},{6,14},{7,15},{8,16},{9,17... | collective-permute-start | bytes 442376 | tf_op jit(solution)/shard_map/ppermute | solution.py:830
  364.9 13.0 %collective-permute-start.16 = (bf16[192,384]{1,0:T(8,128)(2,1)S(1)}, bf16[192,384]{1,0:T(8,128)(2,1)S(1)}, u32[]{:S(2)}, u32[]{:S(2)}) collective-permute-start(bf16[192,384]{1,0:T(8,128)(2,1)S(1)} %add_convert_fusion.1), channel_id=1, source_target_pairs={{0,16},{1,17},{2,18},{3,19},{4,20},{5,21},{6,22},{7,23},{8,24},{9,... | collective-permute-start | bytes 442376 | tf_op jit(solution)/shard_map/ppermute | solution.py:830
  368.3 9.6 %collective-permute-start.17 = (bf16[192,384]{1,0:T(8,128)(2,1)S(1)}, bf16[192,384]{1,0:T(8,128)(2,1)S(1)}, u32[]{:S(2)}, u32[]{:S(2)}) collective-permute-start(bf16[192,384]{1,0:T(8,128)(2,1)S(1)} %add_convert_fusion.1), channel_id=1, source_target_pairs={{0,24},{1,25},{2,26},{3,27},{4,28},{5,29},{6,30},{7,31},{8,0},{9,1... | collective-permute-start | bytes 442376 | tf_op jit(solution)/shard_map/ppermute | solution.py:830
  378.0 9.9 %collective-permute-start.18 = (bf16[4,192,384]{2,1,0:T(8,128)(2,1)S(1)}, bf16[4,192,384]{2,1,0:T(8,128)(2,1)S(1)}, u32[]{:S(2)}, u32[]{:S(2)}) collective-permute-start(bf16[4,192,384]{2,1,0:T(8,128)(2,1)S(1)} %get-tuple-element.105), channel_id=1, source_target_pairs={{0,4},{1,3},{2,6},{3,1},{4,0},{5,7},{6,2},{7,5},{8,12},{9,11},{10,... | collective-permute-start | bytes 1769480 | tf_op jit(solution)/shard_map/ppermute | solution.py:830
  388.1 28.0 %collective-permute-start.19 = (bf16[2,4,192,384]{3,2,1,0:T(8,128)(2,1)S(1)}, bf16[2,4,192,384]{3,2,1,0:T(8,128)(2,1)}, u32[]{:S(2)}, u32[]{:S(2)}) collective-permute-start(bf16[2,4,192,384]{3,2,1,0:T(8,128)(2,1)S(1)} %pad_maximum_fusion.5), channel_id=1, source_target_pairs={{0,2},{1,5},{2,0},{3,7},{4,6},{5,1},{6,4},{7,3},{8,10},{9,13},{10,... | collective-permute-start | bytes 3538952 | tf_op jit(solution)/shard_map/ppermute | solution.py:830
  388.6 42.9 %all-to-all-start.3 = ((bf16[32,192,128]{2,1,0:T(8,128)(2,1)}), bf16[32,192,128]{2,1,0:T(8,128)(2,1)}, u32[]{:S(2)}, u32[]{:S(2)}) async-start(bf16[32,192,128]{2,1,0:T(8,128)(2,1)} %get-tuple-element.86.d_ref), calls=%async_computation.3 | async-start | bytes 3145728 | tf_op jit(solution)/shard_map/all_to_all | solution.py:923
  417.6 20.3 %collective-permute-start.20 = (bf16[4,4,192,384]{3,2,1,0:T(8,128)(2,1)S(1)}, bf16[4,4,192,384]{3,2,1,0:T(8,128)(2,1)}, u32[]{:S(2)}, u32[]{:S(2)}) collective-permute-start(bf16[4,4,192,384]{3,2,1,0:T(8,128)(2,1)S(1)} %pad_maximum_fusion.2), channel_id=1, source_target_pairs={{0,1},{1,0},{2,3},{3,2},{4,5},{5,4},{6,7},{7,6},{8,9},{9,8},{10,11... | collective-permute-start | bytes 7077896 | tf_op jit(solution)/shard_map/ppermute | solution.py:830
  (16 other events, 350.6 us)
Sparse Core Ops, SparseCore 0:
  112.9 63.6 all-gather.1
where the time goes:
time: 479 us; the launch traced here: 473 us
  waiting for transfers between devices  201 us (42%)
  Pallas kernels  147 us (31%)
  starting transfers between devices  73.4 us (15%)
  other arithmetic  24.1 us (5%)
  between operations  15.5 us (3%)
  local copies, waits for them, and re-layouts  11.4 us (2%)
    ppermute x27, waiting for transfers between devices, send(): return lax.ppermute(value, ('frame', 'space'), moves)  146 us
    all_to_all x4, waiting for transfers between devices, swap(): return lax.all_to_all(value, axes, 0, 0, tiled=True)  55.4 us
    ppermute x27, starting transfers between devices, send(): return lax.ppermute(value, ('frame', 'space'), moves)  46.4 us
    pallas_call x3, Pallas kernels, attend_back(): pl.pallas_call(body, out_shape=(jax.ShapeDtypeStruct(out_shape, jnp.bfloa...  36.8 us
    pallas_call x1, Pallas kernels, attend(): pl.pallas_call(body, out_shape=(jax.ShapeDtypeStruct((devices, dim, rows)...  28.7 us
    all_to_all x4, starting transfers between devices, swap(): return lax.all_to_all(value, axes, 0, 0, tiled=True)  26.7 us
    pallas_call x1, Pallas kernels, place_hidden(): pl.pallas_call(body, grid_spec=pltpu.PrefetchScalarGridSpec(num_scalar_pr...  16.9 us
    pallas_call x1, Pallas kernels, hidden_gradients(): pl.pallas_call(body, grid_spec=pltpu.PrefetchScalarGridSpec(num_scalar_pr...  12.4 us
  transfers between devices with their start and end apart: 32, of which 18 were waited for; matrix products, arithmetic and copies ran while one was open for 6% of the time, Pallas kernels for 21%

commit v1 on v0

--- a/solution.py
+++ b/solution.py
@@ -11,8 +11,16 @@
 HEADS = 12
 HEAD_DIM = 64
 VMEM = pl.BlockSpec(memory_space=pltpu.VMEM)
+ANY = pl.BlockSpec(memory_space=pl.ANY)
 SMEM = pl.BlockSpec(memory_space=pltpu.SMEM)
 LIMIT = pltpu.CompilerParams(vmem_limit_bytes=56 * 2**20)
+FLOPS = 1.15e9
+
+
+def busy(microseconds):
+    return pl.CostEstimate(flops=int(microseconds * FLOPS), transcendentals=0, bytes_accessed=0)
+
+
 CLIP = 4
 
 
@@ -117,6 +125,7 @@
         out_specs=(VMEM, VMEM),
         scratch_shapes=[pltpu.VMEM((2, streams, half, rows), jnp.float32)],
         compiler_params=LIMIT,
+        cost_estimate=busy(5),
         name="project",
     )(place, clips, frequencies(rows), block_input, gain[None, :], w_query, w_key, w_value)
 
@@ -141,6 +150,7 @@
         in_specs=[SMEM, VMEM],
         out_specs=VMEM,
         compiler_params=LIMIT,
+        cost_estimate=busy(4),
         name="rope_tables",
     )(lo, frequencies(per_frame))
 
@@ -177,8 +187,13 @@
         in_specs=[VMEM] * 4,
         out_specs=(VMEM, VMEM),
         compiler_params=LIMIT,
+        cost_estimate=busy(3),
         name="attention_out",
     )(attended, block_input, w_out, gain[None, :])
+
+
+def as_row(column):
+    return jnp.broadcast_to(column, (column.shape[0], 128)).T[:1]
 
 
 def whole(shape):
@@ -217,6 +232,7 @@
         ],
         out_specs=(whole((tokens, width)),) * 2,
         compiler_params=LIMIT,
+        cost_estimate=busy(7),
         name="feed_first",
     )(two, cotangent, w_up, w_down)
 
@@ -298,27 +314,22 @@
         out_specs=tuple(whole(shape) for shape, _ in shapes),
         scratch_shapes=[pltpu.VMEM((tokens, width), f32), pltpu.VMEM((tokens, width), f32)],
         compiler_params=LIMIT,
+        cost_estimate=busy(10),
         name="feed_rest",
     )(core, *so_far, attended, middle, two, cotangent, w_out, gain[None, :], w_up, w_down)
 
 
-def out_rows(width, planes):
-    return -(-(width // 4) // (16 * planes)) * 16
-
-
 def hidden_gradients(
-    where, two_mine, two_other, cot_mine, cot_other, w_up, w_down, out_quarter, slots, planes
+    where, two_mine, two_other, cot_mine, cot_other, w_up, w_down, slots, planes
 ):
     pieces, tokens, width = two_mine.shape
     hidden = w_up.shape[1] // slots
     rows = width // planes
-    extra = out_rows(width, planes)
-    quarter = out_quarter.shape[0]
-    height = 2 * rows + extra
+    height = 2 * rows
     low = jnp.bfloat16
 
-    def body(where_ref, two_a, two_b, cot_a, cot_b, up, down, quarter_ref, *rest):
-        outs, (up_sum, down_sum, out_sum) = rest[:planes], rest[planes:]
+    def body(where_ref, two_a, two_b, cot_a, cot_b, up, down, *rest):
+        outs, (up_sum, down_sum) = rest[:planes], rest[planes:]
         step = pl.program_id(0)
 
         def run(two, cot):
@@ -349,16 +360,11 @@
 
         @pl.when(step == pieces - 1)
         def _():
-            out_sum[...] = jnp.zeros_like(out_sum)
-            out_sum[:quarter] = quarter_ref[...]
             for index, out in enumerate(outs):
                 plane = lax.rem(where_ref[1] + index, planes)
                 rows_of = pl.ds(pl.multiple_of(plane * rows, rows), rows)
                 out[:rows] = up_sum[rows_of, :].astype(low)
-                out[rows : 2 * rows] = down_sum[rows_of, :].astype(low)
-                out[2 * rows :] = out_sum[
-                    pl.ds(pl.multiple_of(plane * extra, extra), extra), :
-                ].astype(low)
+                out[rows:] = down_sum[rows_of, :].astype(low)
 
     near = pl.BlockSpec(
         (2, tokens, width), lambda i, where: (jnp.minimum(i, pieces // 2 - 1), 0, 0)
@@ -373,179 +379,121 @@
                 near, far, near, far,
                 pl.BlockSpec((width, hidden), lambda i, where: (0, where[0])),
                 pl.BlockSpec((hidden, width), lambda i, where: (where[0], 0)),
-                whole(out_quarter.shape),
             ],
             out_specs=[whole((height, hidden))] * planes,
             scratch_shapes=[
                 pltpu.VMEM((width, hidden), jnp.float32),
                 pltpu.VMEM((width, hidden), jnp.float32),
-                pltpu.VMEM((extra * planes, hidden), jnp.float32),
             ],
         ),
         out_shape=[jax.ShapeDtypeStruct((height, hidden), low)] * planes,
         compiler_params=LIMIT,
+        cost_estimate=busy(12),
         name="hidden_gradients",
-    )(where, two_mine, two_other, cot_mine, cot_other, w_up, w_down, out_quarter)
-
-
-def place_hidden(where, mine, other, w_up, w_out, gain, slots):
-    spots, planes, height, hidden = mine.shape
+    )(where, two_mine, two_other, cot_mine, cot_other, w_up, w_down)
+
+
+def place_hidden(where, pieces, placed, w_up, gain, planes):
+    spots, height, hidden = pieces.shape
     width = w_up.shape[0]
     rows = width // planes
-    extra = out_rows(width, planes)
-    quarter = width // 4
     f32 = jnp.float32
-
-    def body(where_ref, mine_ref, other_ref, up_ref, gain_ref, up_out, down_out, out, gain_out, low):
+    second = placed is not None
+
+    def body(where_ref, ref, up_ref, gain_ref, *rest):
+        gain_before = rest[2] if second else None
+        up_out, down_out, gain_out, low, sums = rest[3:] if second else rest
         step = pl.program_id(0)
-
-        def put(ref):
-            for index in range(planes):
-                plane = lax.rem(where_ref[3, 0] + planes - index, planes)
-                rows_of = pl.ds(pl.multiple_of(plane * rows, rows), rows)
-                up_out[rows_of, :] = ref[0, index, :rows].astype(f32)
-                low[rows_of, :] = ref[0, index, rows : 2 * rows].astype(f32)
-                row = where_ref[1, step] * quarter + plane * extra
-                rows_of = pl.ds(pl.multiple_of(row, 16), extra)
-                piece = ref[0, index, 2 * rows :].astype(f32)
-
-                @pl.when((plane * extra < quarter) & (where_ref[2, step] == 0))
-                def _():
-                    out[rows_of, :hidden] = piece
-
-                @pl.when((plane * extra < quarter) & (where_ref[2, step] == 1))
-                def _():
-                    out[rows_of, hidden:] = piece
-
-        @pl.when(step < spots)
-        def _():
-            put(mine_ref)
-
-        @pl.when(step >= spots)
-        def _():
-            put(other_ref)
-
+        for index in range(planes):
+            plane = lax.rem(where_ref[1, 0] + planes - index, planes)
+            rows_of = pl.ds(pl.multiple_of(plane * rows, rows), rows)
+            first = 2 * rows * index
+            up_out[rows_of, :] = ref[0, first : first + rows].astype(f32)
+            low[rows_of, :] = ref[0, first + rows : first + 2 * rows].astype(f32)
         down_out[:, :hidden] = low[:hidden]
         down_out[:, hidden:] = low[hidden:]
         terms = jnp.sum(up_out[...] * up_ref[...].astype(f32), axis=1, keepdims=True)
 
         @pl.when(step == 0)
         def _():
-            gain_out[...] = terms
+            sums[...] = terms
 
         @pl.when(step > 0)
         def _():
-            gain_out[...] += terms
-
-        @pl.when(step == slots - 1)
+            sums[...] += terms
+
+        @pl.when(step == spots - 1)
         def _():
-            gain_out[...] /= gain_ref[...]
-
+            row = as_row(sums[...])
+            gain_out[...] = (row + gain_before[...]) / gain_ref[...] if second else row
+
+    unused = [pl.BlockSpec(memory_space=pl.ANY)] * 2 + [whole((1, width))]
     return pl.pallas_call(
         body,
         grid_spec=pltpu.PrefetchScalarGridSpec(
             num_scalar_prefetch=1,
-            grid=(slots,),
+            grid=(spots,),
             in_specs=[
-                pl.BlockSpec(
-                    (1, planes, height, hidden),
-                    lambda i, where: (jnp.minimum(i, spots - 1), 0, 0, 0),
-                ),
-                pl.BlockSpec(
-                    (1, planes, height, hidden),
-                    lambda i, where: (jnp.maximum(i - spots, 0), 0, 0, 0),
-                ),
+                pl.BlockSpec((1, height, hidden), lambda i, where: (i, 0, 0)),
                 pl.BlockSpec((width, hidden), lambda i, where: (0, where[0, i])),
-                whole((width, 1)),
-            ],
+                whole((1, width)),
+            ]
+            + (unused if second else []),
             out_specs=[
                 pl.BlockSpec((width, hidden), lambda i, where: (0, where[0, i])),
                 pl.BlockSpec((hidden, width), lambda i, where: (where[0, i], 0)),
-                whole((width, width)),
-                whole((width, 1)),
+                whole((1, width)),
             ],
-            scratch_shapes=[pltpu.VMEM((width, hidden), f32)],
+            scratch_shapes=[pltpu.VMEM((width, hidden), f32), pltpu.VMEM((width, 1), f32)],
         ),
         out_shape=[
             jax.ShapeDtypeStruct(w_up.shape, f32),
             jax.ShapeDtypeStruct(w_up.shape[::-1], f32),
-            jax.ShapeDtypeStruct(w_out.shape, f32),
-            jax.ShapeDtypeStruct((width, 1), f32),
+            jax.ShapeDtypeStruct((1, width), f32),
         ],
-        compiler_params=LIMIT,
+        input_output_aliases={4: 0, 5: 1} if second else {},
+        compiler_params=LIMIT,
+        cost_estimate=busy(8),
         name="place_hidden",
-    )(where, mine, other, w_up, gain[:, None])
-
-
-def head_products(where, grads, mine, other):
-    devices, height, rows = grads.shape
-    frames, _, width = mine.shape
-    half = width // 2
-
-    def body(where_ref, d_ref, a_ref, b_ref, keep, give, total):
-        core = where_ref[0]
-        total[...] = jnp.zeros_like(total)
-
-        def one(pair, _):
-            lefts, rights = [], []
-            for frame in (2 * pair, 2 * pair + 1):
-                lefts += [d_ref[2 * frame + core], d_ref[2 * frame + 1 - core]]
-                rights += [a_ref[frame], b_ref[frame]]
-            total[...] += dot(
-                jnp.concatenate(lefts, axis=1), jnp.concatenate(rights, axis=0), 1, 0
-            )
-            return 0
-
-        lax.fori_loop(0, frames // 2, one, 0)
-        first = where_ref[1] == 0
-        keep[...] = jnp.where(first, total[:, :half], total[:, half:])
-        give[...] = jnp.where(first, total[:, half:], total[:, :half]).astype(jnp.bfloat16)
-
-    return pl.pallas_call(
-        body,
-        out_shape=(
-            jax.ShapeDtypeStruct((height, half), jnp.float32),
-            jax.ShapeDtypeStruct((height, half), jnp.bfloat16),
-        ),
-        in_specs=[SMEM] + [VMEM] * 3,
-        out_specs=(VMEM, VMEM),
-        scratch_shapes=[pltpu.VMEM((height, width), jnp.float32)],
-        compiler_params=LIMIT,
-        name="head_products",
-    )(where, grads, mine, other)
-
-
-def place_heads(where, mine, other, weights, gain, owners):
-    _, height, half = mine.shape
+    )(where, pieces, w_up, gain[None, :], *(placed or []))
+
+
+def place_heads(pieces, weights, gain, owners):
+    _, height, half = pieces.shape
     width = 2 * half
+    quarter = width // 4
+    size = height - 3 * HEAD_DIM
     f32 = jnp.float32
 
-    def body(where_ref, mine_ref, other_ref, wq, wk, wv, gain_ref, dq, dk, dv, gain_out):
+    def body(ref, wq, wk, wv, gain_ref, dq, dk, dv, out, gain_out):
+        for spot in range(4):
+            for core in range(2):
+                first = (spot if core else spot % 2 * 2 + spot // 2) * quarter
+                columns = slice(core * half, (core + 1) * half)
+                for plane in range(quarter // size):
+                    piece = ref[(plane * 4 + spot) * 2 + core, 3 * HEAD_DIM :]
+                    out[first + plane * size : first + (plane + 1) * size, columns] = piece.astype(f32)
         for side in range(2):
-            blocks = []
-            for head in range(HEADS):
-                entry = where_ref[side, head]
-                own = where_ref[2, 0] == owners[0][head] % 2
-                blocks.append(jnp.where(own, mine_ref[entry], other_ref[entry]))
             rows_of = slice(side * half, (side + 1) * half)
             terms = jnp.zeros((half, 1), f32)
             for kind, (weight, out) in enumerate(((wq, dq), (wk, dk), (wv, dv))):
                 rows = slice(kind * HEAD_DIM, (kind + 1) * HEAD_DIM)
-                flat = jnp.concatenate([block[rows] for block in blocks], axis=0)
+                flat = jnp.concatenate([ref[owner, rows] for owner in owners[side]], axis=0)
                 grad = flat.T.astype(f32)
                 out[rows_of] = grad
                 terms += jnp.sum(grad * weight[rows_of].astype(f32), axis=1, keepdims=True)
-            gain_out[rows_of] = terms / gain_ref[rows_of]
-
-    return pl.pallas_call(
-        body,
-        out_shape=[jax.ShapeDtypeStruct((width, width), f32)] * 3
-        + [jax.ShapeDtypeStruct((width, 1), f32)],
-        in_specs=[SMEM] + [VMEM] * 6,
-        out_specs=[VMEM] * 4,
-        compiler_params=LIMIT,
+            gain_out[:, rows_of] = as_row(terms) / gain_ref[:, rows_of]
+
+    return pl.pallas_call(
+        body,
+        out_shape=[jax.ShapeDtypeStruct((width, width), f32)] * 4
+        + [jax.ShapeDtypeStruct((1, width), f32)],
+        in_specs=[VMEM] * 5,
+        out_specs=[VMEM] * 5,
+        compiler_params=LIMIT,
+        cost_estimate=busy(7),
         name="place_heads",
-    )(where, mine, other, *weights, gain[:, None])
+    )(pieces, *weights, gain[None, :])
 
 
 def input_gradient(grads, weights, block_input, gain, d_middle, owners):
@@ -568,6 +516,7 @@
         in_specs=[VMEM] * 7,
         out_specs=VMEM,
         compiler_params=LIMIT,
+        cost_estimate=busy(6),
         name="input_gradient",
     )(grads, *weights, block_input, gain[None, :], d_middle)
 
@@ -651,6 +600,7 @@
             pltpu.VMEM((CLIP, dim, per_frame), f32),
         ],
         compiler_params=LIMIT,
+        cost_estimate=busy(28),
         name="attend",
     )(lo, packed)
 
@@ -682,11 +632,12 @@
         in_specs=[VMEM] * 3,
         out_specs=(VMEM, VMEM),
         compiler_params=LIMIT,
+        cost_estimate=busy(4),
         name="attend_back_ready",
     )(packed, d_own, out)
 
 
-def attend_back(hi, packed, d_own, lse, delta, kv, qd, tables, d_query, earlier, frames, start, stop):
+def attend_back(hi, packed, d_own, lse, delta, kv, qd, tables, d_query, rest, frames, start, stop):
     devices, _, rows = packed.shape
     spaces = devices // frames
     per_frame = rows * spaces
@@ -697,21 +648,29 @@
     base = 0 if last else start * CLIP * spaces
 
     def body(hi_ref, r_ref, d_ref, lse_ref, delta_ref, kv_ref, qd_ref, table_ref, *rest):
-        rest = list(rest)
-        before = rest.pop(0) if start else None
-        pieces = [rest.pop(0) for _ in earlier] if last else []
-        out = rest.pop(0)
-        d_query_ref, acc, left = rest
+        if last:
+            before, piece, where_ref, near_ref, far_ref, out, keep, give, acc, left, d_query_ref, product, near, far, sems = rest
+        else:
+            out, d_query_ref, acc, left = rest
 
         def begin(frame, _):
-            d_query_ref[frame] = before[frame] if start else jnp.zeros((dim, per_frame), f32)
+            d_query_ref[frame] = jnp.zeros((dim, per_frame), f32)
             return 0
 
-        lax.fori_loop(0, frames, begin, 0)
-        done = 0
-        for piece in pieces:
-            out[done : done + piece.shape[0], dim:, :] = piece[...]
-            done += piece.shape[0]
+        def fetch(pair, slot):
+            return [
+                pltpu.make_async_copy(source.at[pl.ds(2 * pair, 2)], target.at[slot], sems.at[slot, i])
+                for i, (source, target) in enumerate(((near_ref, near), (far_ref, far)))
+            ]
+
+        if last:
+            for copy in fetch(0, 0):
+                copy.start()
+            pltpu.sync_copy(before, d_query_ref)
+        else:
+            lax.fori_loop(0, frames, begin, 0)
+        if last:
+            out[: piece.shape[0], dim:, :] = piece[...]
         first_half = lax.broadcasted_iota(jnp.int32, (per_frame, 2 * dim), 1) < dim
 
         def group(keys, _):
@@ -780,26 +739,69 @@
 
             lax.fori_loop(0, frames, finish, 0)
 
+            core = where_ref[0]
+            product[...] = jnp.zeros_like(product)
+
+            def multiply(pair, _):
+                slot = lax.rem(pair, 2)
+
+                @pl.when(pair + 1 < frames // 2)
+                def _():
+                    for copy in fetch(pair + 1, 1 - slot):
+                        copy.start()
+
+                for copy in fetch(pair, slot):
+                    copy.wait()
+                lefts, rights = [], []
+                for index in range(2):
+                    frame = 2 * pair + index
+                    lefts += [out[spaces * frame + core], out[spaces * frame + 1 - core]]
+                    rights += [near[slot, index], far[slot, index]]
+                product[...] += dot(
+                    jnp.concatenate(lefts, axis=1), jnp.concatenate(rights, axis=0), 1, 0
+                )
+                return 0
+
+            lax.fori_loop(0, frames // 2, multiply, 0)
+            half = product.shape[1] // 2
+            first = where_ref[1] == 0
+            keep[...] = jnp.where(first, product[:, :half], product[:, half:])
+            give[...] = jnp.where(first, product[:, half:], product[:, :half]).astype(jnp.bfloat16)
+
+    inputs = [hi, packed, d_own, lse, delta, kv, qd, tables]
+    in_specs = [SMEM] + [VMEM] * 7
+    query_sum = jax.ShapeDtypeStruct((frames, dim, per_frame), f32)
+    scratch = [
+        pltpu.VMEM((CLIP, 2 * per_frame, 2 * dim), f32),
+        pltpu.VMEM((CLIP, 2 * per_frame, 2 * dim), jnp.bfloat16),
+    ]
     if last:
-        out_shape = (devices, 3 * dim, rows)
+        width = rest[2].shape[2]
+        inputs += [d_query, *rest]
+        in_specs += [ANY, VMEM, SMEM, ANY, ANY]
+        out_shape = (
+            jax.ShapeDtypeStruct((devices, 3 * dim, rows), jnp.bfloat16),
+            jax.ShapeDtypeStruct((3 * dim, width // 2), f32),
+            jax.ShapeDtypeStruct((3 * dim, width // 2), jnp.bfloat16),
+        )
+        scratch += [
+            pltpu.VMEM((frames, dim, per_frame), f32),
+            pltpu.VMEM((3 * dim, width), f32),
+            pltpu.VMEM((2, 2, rows, width), jnp.bfloat16),
+            pltpu.VMEM((2, 2, rows, width), jnp.bfloat16),
+            pltpu.SemaphoreType.DMA((2, 2)),
+        ]
     else:
-        out_shape = ((stop - start) * CLIP * spaces, 2 * dim, rows)
-    inputs = [hi, packed, d_own, lse, delta, kv, qd, tables]
-    inputs += [d_query] if start else []
-    inputs += list(earlier) if last else []
-    return pl.pallas_call(
-        body,
-        out_shape=(
-            jax.ShapeDtypeStruct(out_shape, jnp.bfloat16),
-            jax.ShapeDtypeStruct((frames, dim, per_frame), f32),
-        ),
-        in_specs=[SMEM] + [VMEM] * (len(inputs) - 1),
-        out_specs=(VMEM, VMEM),
-        scratch_shapes=[
-            pltpu.VMEM((CLIP, 2 * per_frame, 2 * dim), f32),
-            pltpu.VMEM((CLIP, 2 * per_frame, 2 * dim), jnp.bfloat16),
-        ],
-        compiler_params=LIMIT,
+        shape = ((stop - start) * CLIP * spaces, 2 * dim, rows)
+        out_shape = (jax.ShapeDtypeStruct(shape, jnp.bfloat16), query_sum)
+    return pl.pallas_call(
+        body,
+        out_shape=out_shape,
+        in_specs=in_specs,
+        out_specs=(VMEM,) * len(out_shape),
+        scratch_shapes=scratch,
+        compiler_params=LIMIT,
+        cost_estimate=busy(20),
         name="attend_back",
     )(*inputs)
 
@@ -842,14 +844,25 @@
         size = self.frames
         return self.send(value, lambda frame, core: ((frame + 4 * step) % size, core))
 
-    def reduce_planes(self, pieces):
-        total = pieces[0].astype(jnp.float32)
-        for step, piece in enumerate(pieces[1:], 1):
-            total = total + self.up(piece, step).astype(jnp.float32)
+    def send_planes(self, pieces):
+        return [self.up(piece, step) for step, piece in enumerate(pieces[1:], 1)]
+
+    def plane_part(self, value):
+        groups = [list(range(spot, self.frames, 4)) for spot in range(4)]
+        if value.shape[0] % (16 * self.planes):
+            return lax.psum(value, "frame", axis_index_groups=groups)
+        return lax.psum_scatter(
+            value, "frame", scatter_dimension=0, axis_index_groups=groups, tiled=True
+        )
+
+    def add_planes(self, own, arrived):
+        total = own.astype(jnp.float32)
+        for piece in arrived:
+            total = total + piece.astype(jnp.float32)
         return total.astype(jnp.bfloat16)
 
     def spread_planes(self, value, count):
-        return jnp.stack([value] + [self.up(value, step) for step in range(1, count)])
+        return [self.up(value, step) for step in range(1, count)]
 
     def gather_spots(self):
         near = jnp.where(self.core == 0, 2, 1)
@@ -858,20 +871,15 @@
         cores = jnp.repeat(jnp.stack([self.core, 1 - self.core]), 4)
         return jnp.concatenate([own, other]), cores
 
-    def gather(self, value):
-        pair = jnp.stack([value, self.second(value)])
+    def gather(self, value, *others):
+        pair = jnp.stack([value, after(self.second(value), *others)])
         return jnp.concatenate([pair, self.first(pair)], axis=0)
 
-    def halve(self, value, bit, exchange):
+    def halves(self, value, bit):
         rows, columns = value.shape
         cut = value.reshape(2, rows // 2, columns)
-        keep = lax.dynamic_index_in_dim(cut, bit, 0, keepdims=False)
-        give = lax.dynamic_index_in_dim(cut, 1 - bit, 0, keepdims=False)
-        return keep + exchange(give.astype(jnp.bfloat16)).astype(jnp.float32)
-
-
-def quarter_rows(spots, cores):
-    return jnp.where(cores == 1, spots, (spots % 2) * 2 + spots // 2)
+        pick = lambda index: lax.dynamic_index_in_dim(cut, index, 0, keepdims=False)
+        return pick(bit), pick(1 - bit).astype(jnp.bfloat16)
 
 
 def frame_limits(clip_frames, frames):
@@ -910,28 +918,27 @@
 
     owners = head_owners(frames, spaces)
     w_projections = (w_query, w_key, w_value)
-
-    begin, end = frame_limits(clip_frames, frames)
+    side = ring.frame % 2
+
+    def swap(value):
+        return lax.all_to_all(value, axes, 0, 0, tiled=True)
+
+    spot_of = jnp.stack([ring.frame, ring.core * rows])
+    sent, normed = project(
+        spot_of, clip_frames, block_input, norm1_gain, *w_projections, owners, devices, per_frame
+    )
+    packed = swap(sent)
+
+    begin, end = frame_limits(after(clip_frames, sent), frames)
     frame_ids = jnp.arange(frames, dtype=jnp.int32)
     mine = ring.frame * spaces + ring.core
     idle = ~jnp.any(mine == jnp.asarray(owners))
-    side = ring.frame % 2
     lo = jnp.where(idle, frame_ids, jnp.where(side == 0, begin[0], begin[1]))
     hi = jnp.where(idle, frame_ids, jnp.where(side == 0, end[0], end[1]))
 
-    def swap(value):
-        return lax.all_to_all(value, axes, 0, 0, tiled=True)
-
-    spot_of = jnp.stack([ring.frame, ring.core * rows])
-    sent, normed = project(
-        spot_of, clip_frames, block_input, norm1_gain, *w_projections, owners, devices, per_frame
-    )
-    packed = swap(sent)
-    tables = rope_tables(after(lo, sent), frames, per_frame)
     neighbour = lambda value: ring.send(value, lambda frame, core: (frame ^ 1, core))
-    normed_later = after(normed, packed)
-    stream_near = neighbour(lax.dynamic_index_in_dim(normed_later, 1 - side, 0))
-    stream_own = lax.dynamic_index_in_dim(normed_later, side, 0)
+    stream_near = neighbour(lax.dynamic_index_in_dim(normed, 1 - side, 0))
+    stream_own = lax.dynamic_index_in_dim(normed, side, 0)
     stream_pair = jnp.where(
         side == 0,
         jnp.concatenate([stream_own, stream_near]),
@@ -942,82 +949,80 @@
         stream_pair, "frame", axis=0, tiled=True, axis_index_groups=same_side
     )
     cot_flat = cotangent.reshape(tokens, width)
-    cot_one = ring.second(after(cot_flat, packed))
-    out, out_low, lse, kv = attend(lo, packed, frames)
-    attended = swap(out_low)
-    cot_pair = after(jnp.stack([cot_flat, cot_one]), out_low)
-    cot_mine = jnp.concatenate([cot_pair, ring.first(cot_pair)], axis=0)
+    cot_one = ring.second(cot_flat)
+    out, out_low, lse, kv = attend(lo, after(packed, stream_pair), frames)
+    cot_pair = jnp.stack([cot_flat, after(cot_one, out_low)])
+    attended = swap(after(out_low, cot_pair))
+    cot_far = ring.first(cot_pair)
 
     middle, two = attention_out(attended, block_input, w_out, norm2_gain, owners)
-    cot_other = ring.across(after(cot_mine, middle))
     chunk, skip = 512, 3
+    cot_mine = jnp.concatenate([cot_pair, after(cot_far, middle)], axis=0)
+    cot_other = ring.across(cot_mine)
     so_far = feed_first(two, cotangent, w_up, w_down, chunk, skip)
     two_pair = jnp.stack([two, ring.second(two)])
-    so_far = after(so_far, two_pair)
-    two_mine = jnp.concatenate([two_pair, ring.first(two_pair)], axis=0)
+    so_far = after(so_far, two_pair, stream_mine)
+    two_far = ring.first(two_pair)
     block_output, d_middle, d_sent, out_keep, out_give = feed_rest(
         core, so_far, attended, middle, two, cotangent, w_out, norm2_gain, w_up, w_down,
         chunk, skip, owners,
     )
     d_own = swap(d_sent)
+    tables = rope_tables(after(lo, d_sent), frames, per_frame)
+    two_mine = jnp.concatenate([two_pair, after(two_far, d_sent)], axis=0)
     two_other = ring.across(two_mine)
-    out_sum = out_keep + ring.across(out_give).astype(jnp.float32)
-    out_sum = ring.halve(out_sum, ring.first_bit, ring.first)
-    out_sum = ring.halve(out_sum, ring.second_bit, ring.second)
+    out_other = ring.across(out_give)
     pieces = hidden_gradients(
         jnp.stack([ring.spot * spaces + ring.core, ring.plane]),
-        two_mine, two_other, cot_mine, cot_other, w_up, w_down, out_sum, slots, planes,
-    )
-
-    total = ring.reduce_planes(pieces)
+        two_mine, two_other, cot_mine, cot_other, w_up, w_down, slots, planes,
+    )
+
+    arrived = ring.send_planes(pieces)
+    out_sum = out_keep + after(out_other, pieces[0]).astype(jnp.float32)
+    out_keep, out_give = ring.halves(out_sum, ring.first_bit)
+    out_other = ring.first(out_give)
+    qd, delta = attend_back_ready(packed, d_own, out, frames)
+    out_sum = out_keep + after(out_other, qd).astype(jnp.float32)
+    out_keep, out_give = ring.halves(out_sum, ring.second_bit)
+    out_sum = (out_keep + ring.second(out_give).astype(jnp.float32)).astype(low)
+    delta = after(delta, out_sum)
+    out_sum = ring.plane_part(out_sum)
+    groups = frames // CLIP
+    first_part, d_query = attend_back(
+        hi, packed, d_own, lse, delta, kv, qd, tables, None, None, frames, 0, groups // 2
+    )
+    total = ring.add_planes(pieces[0], after(arrived, first_part))
     stream_other = ring.across(stream_mine)
-    qd, delta = attend_back_ready(packed, after(d_own, pieces[0]), out, frames)
-    groups = frames // CLIP
-    cuts = [0, groups // 4, groups // 2, groups]
-    d_query, earlier = None, []
-    for start, stop in zip(cuts[:-1], cuts[1:]):
-        delta_now = after(delta, total) if stop == groups else delta
-        result, d_query = attend_back(
-            hi, packed, d_own, lse, delta_now, kv, qd, tables, d_query, earlier, frames, start, stop
-        )
-        earlier.append(result)
-    hidden_mine = ring.gather(ring.spread_planes(total, planes))
-    back = swap(result)
+    grads, keep, give = attend_back(
+        hi, packed, d_own, lse, after(delta, total), kv, qd, tables, d_query,
+        (first_part, jnp.stack([ring.core, side]), stream_mine, stream_other),
+        frames, groups // 2, groups,
+    )
+    spread = after(ring.spread_planes(total, planes), keep)
+    back = swap(after(grads, spread))
+    heads_sum = (keep + neighbour(give).astype(jnp.float32)).astype(low)
+    heads_all = lax.all_gather(jnp.concatenate([heads_sum, out_sum]), axes)
+    hidden_mine = ring.gather(after(jnp.concatenate([total, *spread]), heads_sum), back)
     hidden_other = ring.across(hidden_mine)
+    grad_input = input_gradient(back, w_projections, block_input, norm1_gain, d_middle, owners)
     unit_slots = spots * spaces + cores
-    where = jnp.stack(
-        [unit_slots, quarter_rows(spots, cores), cores, jnp.broadcast_to(ring.plane, cores.shape)]
-    )
-    grad_up, grad_down, grad_out, gain_two = place_hidden(
-        where, hidden_mine, hidden_other, w_up, w_out, norm2_gain, slots
-    )
-
-    keep, give = head_products(jnp.stack([ring.core, side]), result, stream_mine, stream_other)
-    heads_sum = (keep + neighbour(give).astype(jnp.float32)).astype(low)
-    heads_mine = ring.gather(ring.spread_planes(heads_sum, planes))
-    heads_other = ring.across(heads_mine)
-    owner_of = jnp.asarray([[owners[stream][head] for head in range(HEADS)] for stream in range(2)])
-    owner_plane, owner_spot = owner_of // (4 * spaces), owner_of // spaces % 4
-    owner_core = owner_of % spaces
-    list_of = jnp.where(owner_core == ring.core, 0, 1)
-    entries = jnp.stack([spots[:4], spots[4:]])[list_of] == owner_spot[..., None]
-    entry = jnp.sum(jnp.where(entries, jnp.arange(4), 0), axis=-1)
-    entry = entry * planes + (ring.plane - owner_plane) % planes
-    where = jnp.concatenate([entry, jnp.broadcast_to(ring.core, (1, HEADS))]).astype(jnp.int32)
-    flat = lambda value: value.reshape((-1,) + value.shape[2:])
-    grad_query, grad_key, grad_value, gain_one = place_heads(
-        where, flat(heads_mine), flat(heads_other), w_projections, norm1_gain, owners
-    )
-    grad_input = input_gradient(back, w_projections, block_input, norm1_gain, d_middle, owners)
+    where = jnp.stack([unit_slots, jnp.broadcast_to(ring.plane, cores.shape)])
+    placed = place_hidden(where[:, :4], hidden_mine, None, w_up, norm2_gain, planes)
+    grad_up, grad_down, gain_two = place_hidden(
+        where[:, 4:], after(hidden_other, placed[0], grad_input), placed, w_up, norm2_gain, planes
+    )
+    grad_query, grad_key, grad_value, grad_out, gain_one = place_heads(
+        after(heads_all, grad_up), w_projections, norm1_gain, owners
+    )
     return (
         block_output,
         grad_input,
-        gain_one.reshape(width),
+        gain_one[0],
         grad_query,
         grad_key,
         grad_value,
         grad_out,
-        gain_two.reshape(width),
+        gain_two[0],
         grad_up,
         grad_down,
     )

time: 479 us -> 368 us (0.77)
  waiting for transfers between devices: 201 us -> 147 us
  Pallas kernels: 147 us -> 111 us
  other arithmetic: 24.1 us -> 14.5 us
  local copies, waits for them, and re-layouts: 11.4 us -> 6.49 us
    ppermute x27 -> x21, waiting for transfers between devices: 146 us -> 85.2 us  [send(): return lax.ppermute(value, ('frame', 'space'), moves)]
    pallas_call x4 -> x2, Pallas kernels: 43.5 us -> 23.4 us  [attend_back(): pl.pallas_call(body, out_shape=out_shape, in_specs=in_specs, out_specs=(V...]
    pallas_call x1, Pallas kernels: 28.7 us -> 11.5 us  [attend(): pl.pallas_call(body, out_shape=(jax.ShapeDtypeStruct((devices, dim, rows)...]
    ppermute x27 -> x21, starting transfers between devices: 46.4 us -> 32.8 us  [send(): return lax.ppermute(value, ('frame', 'space'), moves)]
    all_to_all x4, starting transfers between devices: 26.7 us -> 39.1 us  [swap(): return lax.all_to_all(value, axes, 0, 0, tiled=True)]
    reduce_scatter x0 -> x1, waiting for transfers between devices: none -> 10.3 us  [plane_part(): lax.psum_scatter(value, 'frame', scatter_dimension=0, axis_index_groups=g...]
    pallas_call x1 -> x2, Pallas kernels: 16.9 us -> 17 us  [place_hidden(): pl.pallas_call(body, grid_spec=pltpu.PrefetchScalarGridSpec(num_scalar_pr...]
  transfers between devices with their start and end apart: 32 -> 28, of which waited for: 18 -> 11; matrix products, arithmetic and copies ran while one was open for 6% -> 4% of each run, Pallas kernels for 21% -> 27%
where the time goes in v1:
time: 368 us; the launch traced here: 366 us
  waiting for transfers between devices  147 us (40%)
  Pallas kernels  111 us (30%)
  starting transfers between devices  72 us (20%)
  between operations  14.8 us (4%)
  other arithmetic  14.5 us (4%)
  local copies, waits for them, and re-layouts  6.49 us (2%)
    ppermute x21, waiting for transfers between devices, send(): return lax.ppermute(value, ('frame', 'space'), moves)  85.2 us
    all_to_all x4, waiting for transfers between devices, swap(): return lax.all_to_all(value, axes, 0, 0, tiled=True)  51.1 us
    all_to_all x4, starting transfers between devices, swap(): return lax.all_to_all(value, axes, 0, 0, tiled=True)  39.1 us
    ppermute x21, starting transfers between devices, send(): return lax.ppermute(value, ('frame', 'space'), moves)  32.8 us
    pallas_call x2, Pallas kernels, attend_back(): pl.pallas_call(body, out_shape=out_shape, in_specs=in_specs, out_specs=(V...  23.4 us
    pallas_call x2, Pallas kernels, place_hidden(): pl.pallas_call(body, grid_spec=pltpu.PrefetchScalarGridSpec(num_scalar_pr...  17 us
    pallas_call x1, Pallas kernels, hidden_gradients(): pl.pallas_call(body, grid_spec=pltpu.PrefetchScalarGridSpec(num_scalar_pr...  12.2 us
    pallas_call x1, Pallas kernels, attend(): pl.pallas_call(body, out_shape=(jax.ShapeDtypeStruct((devices, dim, rows)...  11.5 us
  transfers between devices with their start and end apart: 28, of which 11 were waited for; matrix products, arithmetic and copies ran while one was open for 4% of the time, Pallas kernels for 27%

profile of v1, /device:TPU:0, one launch (start us, length us, event | category | flops | bytes accessed | tf_op | source)
XLA Modules:
  0.0 365.7 jit_solution(3301486028468579300)
XLA Ops:
  9.0 4.7 %project.1 = (bf16[32,192,128]{2,1,0:T(8,128)(2,1)}, bf16[2,128,768]{2,1,0:T(8,128)(2,1)}) custom-call(s32[2]{0:T(128)} %pad_add_fusion.place_ref, s32[2,4]{1,0:T(2,128)} %clips_ref.1, f32[32,128]{1,0:T(8,128)} %constant.94.clone.freq_ref, bf16[2,128,768]{2,1,0:T(8,128)(2,1)} %x_ref.5, f32[1,768]{1,0:T(1,128)} %broadcast_in_dim.20.gain_ref, ...), custom_call_target="tpu_custom_call" | custom-call | flops 5750000128 | tf_op jit(solution)/shard_map/project/pallas_call | solution.py:118
  13.7 7.3 %all-to-all-start = ((bf16[32,192,128]{2,1,0:T(8,128)(2,1)}), bf16[32,192,128]{2,1,0:T(8,128)(2,1)S(1)}, u32[]{:S(2)}, u32[]{:S(2)}) async-start(bf16[32,192,128]{2,1,0:T(8,128)(2,1)} %get-tuple-element.71), calls=%async_computation | async-start | bytes 3145728 | tf_op jit(solution)/shard_map/all_to_all | solution.py:924
  21.2 1.8 collective-permute-start
  26.6 13.0 %collective-permute-done = bf16[1,128,768]{2,1,0:T(8,128)(2,1)S(1)} collective-permute-done((bf16[1,128,768]{2,1,0:T(8,128)(2,1)S(1)}, bf16[1,128,768]{2,1,0:T(8,128)(2,1)S(1)}, u32[]{:S(2)}, u32[]{:S(2)}) %collective-permute-start) | collective-permute-done | bytes 196640 | tf_op jit(solution)/shard_map/ppermute | solution.py:832
  40.4 30.5 %all-to-all-done.r_ref = bf16[32,192,128]{2,1,0:T(8,128)(2,1)S(1)} async-done(((bf16[32,192,128]{2,1,0:T(8,128)(2,1)}), bf16[32,192,128]{2,1,0:T(8,128)(2,1)S(1)}, u32[]{:S(2)}, u32[]{:S(2)}) %all-to-all-start) | async-done | bytes 1572896 | tf_op jit(solution)/shard_map/all_to_all | solution.py:924
  72.0 11.5 %attend.1 = (f32[32,64,128]{2,1,0:T(8,128)}, bf16[32,64,128]{2,1,0:T(8,128)(2,1)}, f32[16,1,256]{2,1,0:T(1,128)}, bf16[4096,128]{1,0:T(8,128)(2,1)}) custom-call(s32[16]{0:T(128)} %broadcast_select_fusion.3.lo_ref, bf16[32,192,128]{2,1,0:T(8,128)(2,1)} %copy-done), custom_call_target="tpu_custom_call" | custom-call | flops 32199999488 | tf_op jit(solution)/shard_map/attend/pallas_call | solution.py:587
  83.6 20.0 %all-to-all-start.1 = ((bf16[32,64,128]{2,1,0:T(8,128)(2,1)}), bf16[32,64,128]{2,1,0:T(8,128)(2,1)S(1)}, u32[]{:S(2)}, u32[]{:S(2)}) async-start(bf16[32,64,128]{2,1,0:T(8,128)(2,1)} %get-tuple-element.77), calls=%async_computation.1 | async-start | bytes 1048576 | tf_op jit(solution)/shard_map/all_to_all | solution.py:924
  103.6 1.8 collective-permute-start.6
  106.0 13.2 %all-to-all-done.1.att = bf16[32,64,128]{2,1,0:T(8,128)(2,1)S(1)} async-done(((bf16[32,64,128]{2,1,0:T(8,128)(2,1)}), bf16[32,64,128]{2,1,0:T(8,128)(2,1)S(1)}, u32[]{:S(2)}, u32[]{:S(2)}) %all-to-all-start.1) | async-done | bytes 524320 | tf_op jit(solution)/shard_map/all_to_all | solution.py:924
  120.0 3.1 attention_out.1
  125.3 6.6 %feed_first.1 = (f32[256,768]{1,0:T(8,128)}, f32[256,768]{1,0:T(8,128)}) custom-call(bf16[256,768]{1,0:T(8,128)(2,1)} %get-tuple-element.78.two_ref, bf16[2,128,768]{2,1,0:T(8,128)(2,1)} %cot.3, bf16[768,3072]{1,0:T(8,128)(2,1)} %up_ref.3, bf16[3072,768]{1,0:T(8,128)(2,1)} %down.5), custom_call_target="tpu_custom_call" | custom-call | flops 8049999872 | tf_op jit(solution)/shard_map/feed_first/pallas_call | solution.py:224
  133.3 10.3 %feed_rest.1 = (bf16[2,128,768]{2,1,0:T(8,128)(2,1)}, f32[256,768]{1,0:T(8,128)}, bf16[32,64,128]{2,1,0:T(8,128)(2,1)}, f32[768,384]{1,0:T(8,128)}, bf16[768,384]{1,0:T(8,128)(2,1)}) custom-call(s32[1]{0:T(128)} %bitcast.core_ref, f32[256,768]{1,0:T(8,128)} %get-tuple-element.81.first_result, f32[256,768]{1,0:T(8,128)} %get-tuple-element.82.first_two, ...), custom_call_target="tpu_custom_call" | custom-call | flops 11500000256 | tf_op jit(solution)/shard_map/feed_rest/pallas_call | solution.py:303
  148.5 3.5 all-to-all-start.2
  152.7 12.2 %hidden_gradients.1 = (bf16[384,384]{1,0:T(8,128)(2,1)}, bf16[384,384]{1,0:T(8,128)(2,1)}, bf16[384,384]{1,0:T(8,128)(2,1)}, bf16[384,384]{1,0:T(8,128)(2,1)}) custom-call(s32[2]{0:T(128)} %pad_add_fusion.1.where_ref, bf16[4,256,768]{2,1,0:T(8,128)(2,1)} %copy-done.2, bf16[4,256,768]{2,1,0:T(8,128)(2,1)} %collective-permute-done.5.two_b, ...), custom_call_target="tpu_custom_call" | custom-call | flops 13799999488 | tf_op jit(solution)/shard_map/hidden_gradients/pallas_call | solution.py:373
  167.6 3.6 attend_back_ready.1
  173.6 3.9 %rope_tables.1.table_ref = f32[16,2,32,256]{3,2,1,0:T(8,128)} custom-call(s32[16]{0:T(128)} %broadcast_select_fusion.3.lo_ref, f32[32,256]{1,0:T(8,128)} %constant.96.clone.freq_ref), custom_call_target="tpu_custom_call" | custom-call | flops 4600000000 | tf_op jit(solution)/shard_map/rope_tables/pallas_call | solution.py:147
  179.0 2.5 collective-permute-start.11
  183.6 7.8 %attend_back.2 = (bf16[16,128,128]{2,1,0:T(8,128)(2,1)}, f32[16,64,256]{2,1,0:T(8,128)}) custom-call(s32[16]{0:T(128)} %broadcast_select_fusion.2.hi_ref, bf16[32,192,128]{2,1,0:T(8,128)(2,1)} %copy-done, bf16[32,64,128]{2,1,0:T(8,128)(2,1)} %all-to-all-done.2.d_ref, f32[16,1,256]{2,1,0:T(1,128)} %get-tuple-element.86.lse_ref, ...), custom_call_target="tpu_custom_call" | custom-call | flops 23000000512 | tf_op jit(solution)/shard_map/attend_back/pallas_call | solution.py:797
  191.4 8.6 %collective-permute-done.11 = bf16[384,384]{1,0:T(8,128)(2,1)S(1)} collective-permute-done((bf16[384,384]{1,0:T(8,128)(2,1)S(1)}, bf16[384,384]{1,0:T(8,128)(2,1)S(1)}, u32[]{:S(2)}, u32[]{:S(2)}) %collective-permute-start.11) | collective-permute-done | bytes 294944 | tf_op jit(solution)/shard_map/ppermute | solution.py:832
  200.1 6.8 %collective-permute-start.14 = (bf16[384,384]{1,0:T(8,128)(2,1)S(1)}, bf16[384,384]{1,0:T(8,128)(2,1)S(1)}, u32[]{:S(2)}, u32[]{:S(2)}) collective-permute-start(bf16[384,384]{1,0:T(8,128)(2,1)S(1)} %add_convert_fusion), channel_id=1, source_target_pairs={{0,8},{1,9},{2,10},{3,11},{4,12},{5,13},{6,14},{7,15},{8,16},{9,17... | collective-permute-start | bytes 884744 | tf_op jit(solution)/shard_map/ppermute | solution.py:832
  209.4 15.6 %attend_back.3 = (bf16[32,192,128]{2,1,0:T(8,128)(2,1)}, f32[192,384]{1,0:T(8,128)}, bf16[192,384]{1,0:T(8,128)(2,1)}) custom-call(s32[16]{0:T(128)} %broadcast_select_fusion.2.hi_ref, bf16[32,192,128]{2,1,0:T(8,128)(2,1)} %copy-done, bf16[32,64,128]{2,1,0:T(8,128)(2,1)} %all-to-all-done.2.d_ref, f32[16,1,256]{2,1,0:T(1,128)} %get-tuple-element.86.lse_ref, ...), custom_call_target="tpu_custom_call" | custom-call | flops 23000000512 | tf_op jit(solution)/shard_map/attend_back/pallas_call | solution.py:797
  225.0 3.6 collective-permute-start.17
  228.6 8.3 %all-to-all-start.3 = ((bf16[32,192,128]{2,1,0:T(8,128)(2,1)}), bf16[32,192,128]{2,1,0:T(8,128)(2,1)}, u32[]{:S(2)}, u32[]{:S(2)}) async-start(bf16[32,192,128]{2,1,0:T(8,128)(2,1)} %get-tuple-element.114), calls=%async_computation.3 | async-start | bytes 3145728 | tf_op jit(solution)/shard_map/all_to_all | solution.py:924
  237.0 10.3 %reduce-scatter.2.cloned.1.call-done = bf16[48,384]{1,0:T(8,128)(2,1)} async-done(((bf16[192,384]{1,0:T(8,128)(2,1)}), bf16[48,384]{1,0:T(8,128)(2,1)}) %reduce-scatter.2.cloned.1.call-update) | async-done | bytes 36880 | tf_op jit(solution)/shard_map/reduce_scatter | solution.py:854
  250.4 22.1 %collective-permute-done.18 = bf16[1536,384]{1,0:T(8,128)(2,1)S(1)} collective-permute-done((bf16[1536,384]{1,0:T(8,128)(2,1)S(1)}, bf16[1536,384]{1,0:T(8,128)(2,1)S(1)}, u32[]{:S(2)}, u32[]{:S(2)}) %collective-permute-start.18) | collective-permute-done | bytes 1179680 | tf_op jit(solution)/shard_map/ppermute | solution.py:832
  272.5 6.6 %all-to-all-done.3.d_ref = bf16[32,192,128]{2,1,0:T(8,128)(2,1)} async-done(((bf16[32,192,128]{2,1,0:T(8,128)(2,1)}), bf16[32,192,128]{2,1,0:T(8,128)(2,1)}, u32[]{:S(2)}, u32[]{:S(2)}) %all-to-all-start.3) | async-done | bytes 1572896 | tf_op jit(solution)/shard_map/all_to_all | solution.py:924
  280.9 40.3 %collective-permute-done.19 = bf16[2,1536,384]{2,1,0:T(8,128)(2,1)S(1)} collective-permute-done((bf16[2,1536,384]{2,1,0:T(8,128)(2,1)S(1)}, bf16[2,1536,384]{2,1,0:T(8,128)(2,1)S(1)}, u32[]{:S(2)}, u32[]{:S(2)}) %collective-permute-start.19) | collective-permute-done | bytes 2359328 | tf_op jit(solution)/shard_map/ppermute | solution.py:832
  321.2 2.5 pad_maximum_fusion.ref
  324.6 6.5 %input_gradient.1 = f32[2,128,768]{2,1,0:T(8,128)} custom-call(bf16[32,192,128]{2,1,0:T(8,128)(2,1)} %all-to-all-done.3.d_ref, bf16[768,768]{1,0:T(8,128)(2,1)} %wq.5, bf16[768,768]{1,0:T(8,128)(2,1)} %wk.5, bf16[768,768]{1,0:T(8,128)(2,1)} %wv.5, bf16[2,128,768]{2,1,0:T(8,128)(2,1)} %x_ref.5, f32[1,768]{1,0:T(1,128)} %broadcast_in_dim.20.gain_ref, ...), custom_call_target="tpu_custom_call" | custom-call | flops 6899999744 | tf_op jit(solution)/shard_map/input_gradient/pallas_call | solution.py:513
  331.2 8.5 %place_hidden.2 = (f32[768,3072]{1,0:T(8,128)}, f32[3072,768]{1,0:T(8,128)}, f32[1,768]{1,0:T(1,128)}) custom-call(s32[2,4]{1,0:T(2,128)} %get-tuple-element.136.where_ref, bf16[4,1536,384]{2,1,0:T(8,128)(2,1)} %pad_maximum_fusion.ref, bf16[768,3072]{1,0:T(8,128)(2,1)} %up_ref.3, f32[1,768]{1,0:T(1,128)} %broadcast_in_dim.35.gain_ref), custom_call_target="tpu_custom_call" | custom-call | flops 9200000000 | tf_op jit(solution)/shard_map/place_hidden/pallas_call | solution.py:431
  339.6 8.5 %place_hidden.3 = (f32[768,3072]{1,0:T(8,128)}, f32[3072,768]{1,0:T(8,128)}, f32[1,768]{1,0:T(1,128)}) custom-call(s32[2,4]{1,0:T(2,128)} %get-tuple-element.137.where_ref, bf16[4,1536,384]{2,1,0:T(8,128)(2,1)} %collective-permute-done.20.ref, bf16[768,3072]{1,0:T(8,128)(2,1)} %up_ref.3, ...), custom_call_target="tpu_custom_call", output_to_operand_aliasing={{0}: (4, {}), {1}: (5, {})} | custom-call | flops 9200000000 | tf_op jit(solution)/shard_map/place_hidden/pallas_call | solution.py:431
  349.4 8.5 %place_heads.1 = (f32[768,768]{1,0:T(8,128)}, f32[768,768]{1,0:T(8,128)}, f32[768,768]{1,0:T(8,128)}, f32[768,768]{1,0:T(8,128)}, f32[1,768]{1,0:T(1,128)}) custom-call(bf16[32,240,384]{2,1,0:T(8,128)(2,1)} %bitcast.56, bf16[768,768]{1,0:T(8,128)(2,1)} %wq.5, bf16[768,768]{1,0:T(8,128)(2,1)} %wk.5, bf16[768,768]{1,0:T(8,128)(2,1)} %wv.5, ...), custom_call_target="tpu_custom_call" | custom-call | flops 8049999872 | tf_op jit(solution)/shard_map/place_heads/pallas_call | solution.py:487
  (115 shorter events, 37.0 us)
Async XLA Ops:
  13.7 57.1 %all-to-all-start = ((bf16[32,192,128]{2,1,0:T(8,128)(2,1)}), bf16[32,192,128]{2,1,0:T(8,128)(2,1)S(1)}, u32[]{:S(2)}, u32[]{:S(2)}) async-start(bf16[32,192,128]{2,1,0:T(8,128)(2,1)} %get-tuple-element.71), calls=%async_computation | async-start | bytes 3145728 | tf_op jit(solution)/shard_map/all_to_all | solution.py:924
  21.1 112.2 %all-gather.4.cloned.1.call-start = ((), (), s32[]{:S(2)}) async-start(), calls=%async_computation.5 | async-start | bytes 3538944 | tf_op jit(solution)/shard_map/all_gather | solution.py:948
  21.2 18.4 %collective-permute-start = (bf16[1,128,768]{2,1,0:T(8,128)(2,1)S(1)}, bf16[1,128,768]{2,1,0:T(8,128)(2,1)S(1)}, u32[]{:S(2)}, u32[]{:S(2)}) collective-permute-start(bf16[1,128,768]{2,1,0:T(8,128)(2,1)S(1)} %get-tuple-element.135), channel_id=1, source_target_pairs={{0,2},{1,3},{2,0},{3,1},{4,6},{5,7},{6,4},{7,5},{8,10},{9,11},{10,... | collective-permute-start | bytes 589832 | tf_op jit(solution)/shard_map/ppermute | solution.py:832
  23.0 60.5 %collective-permute-start.1 = (bf16[256,768]{1,0:T(8,128)(2,1)S(1)}, bf16[256,768]{1,0:T(8,128)(2,1)S(1)}, u32[]{:S(2)}, u32[]{:S(2)}) collective-permute-start(bf16[256,768]{1,0:T(8,128)(2,1)S(1)} %bitcast.47), channel_id=1, source_target_pairs={{0,4},{1,3},{2,6},{3,1},{4,0},{5,7},{6,2},{7,5},{8,12},{9,11},{10,... | collective-permute-start | bytes 1179656 | tf_op jit(solution)/shard_map/ppermute | solution.py:832
  83.5 22.0 %copy-start.13 = (f32[768]{0:T(1024)S(1)}, f32[768]{0:T(1024)}, u32[]{:S(2)}) copy-start(f32[768]{0:T(1024)} %param.20) | copy-start | bytes 9220
  83.6 35.6 %all-to-all-start.1 = ((bf16[32,64,128]{2,1,0:T(8,128)(2,1)}), bf16[32,64,128]{2,1,0:T(8,128)(2,1)S(1)}, u32[]{:S(2)}, u32[]{:S(2)}) async-start(bf16[32,64,128]{2,1,0:T(8,128)(2,1)} %get-tuple-element.77), calls=%async_computation.1 | async-start | bytes 1048576 | tf_op jit(solution)/shard_map/all_to_all | solution.py:924
  103.6 19.5 %collective-permute-start.6 = (bf16[2,256,768]{2,1,0:T(8,128)(2,1)S(1)}, bf16[2,256,768]{2,1,0:T(8,128)(2,1)S(1)}, u32[]{:S(2)}, u32[]{:S(2)}) collective-permute-start(bf16[2,256,768]{2,1,0:T(8,128)(2,1)S(1)} %pad_maximum_fusion.5), channel_id=1, source_target_pairs={{0,2},{1,5},{2,0},{3,7},{4,6},{5,1},{6,4},{7,3},{8,10},{9,13},{10,... | collective-permute-start | bytes 2359304 | tf_op jit(solution)/shard_map/ppermute | solution.py:832
  123.3 29.4 %collective-permute-start.7 = (bf16[4,256,768]{2,1,0:T(8,128)(2,1)S(1)}, bf16[4,256,768]{2,1,0:T(8,128)(2,1)}, u32[]{:S(2)}, u32[]{:S(2)}) collective-permute-start(bf16[4,256,768]{2,1,0:T(8,128)(2,1)S(1)} %pad_maximum_fusion.3.cot_a), channel_id=1, source_target_pairs={{0,1},{1,0},{2,3},{3,2},{4,5},{5,4},{6,7},{7,6},{8,9},{9,8},{10,11... | collective-permute-start | bytes 4718600 | tf_op jit(solution)/shard_map/ppermute | solution.py:832
  124.1 7.8 %collective-permute-start.2 = (bf16[256,768]{1,0:T(8,128)(2,1)S(1)}, bf16[256,768]{1,0:T(8,128)(2,1)S(1)}, u32[]{:S(2)}, u32[]{:S(2)}) collective-permute-start(bf16[256,768]{1,0:T(8,128)(2,1)S(1)} %copy-done.4), channel_id=1, source_target_pairs={{0,4},{1,3},{2,6},{3,1},{4,0},{5,7},{6,2},{7,5},{8,12},{9,11},{10,... | collective-permute-start | bytes 1179656 | tf_op jit(solution)/shard_map/ppermute | solution.py:832
  132.0 12.1 %collective-permute-start.4 = (bf16[2,256,768]{2,1,0:T(8,128)(2,1)S(1)}, bf16[2,256,768]{2,1,0:T(8,128)(2,1)S(1)}, u32[]{:S(2)}, u32[]{:S(2)}) collective-permute-start(bf16[2,256,768]{2,1,0:T(8,128)(2,1)S(1)} %pad_maximum_fusion.6), channel_id=1, source_target_pairs={{0,2},{1,5},{2,0},{3,7},{4,6},{5,1},{6,4},{7,3},{8,10},{9,13},{10,... | collective-permute-start | bytes 2359304 | tf_op jit(solution)/shard_map/ppermute | solution.py:832
  133.3 11.7 %copy-start.6 = (bf16[256,768]{1,0:T(8,128)(2,1)S(1)}, bf16[256,768]{1,0:T(8,128)(2,1)}, u32[]{:S(2)}) copy-start(bf16[256,768]{1,0:T(8,128)(2,1)} %get-tuple-element.78.two_ref) | copy-start | bytes 1179652
  146.3 6.4 %collective-permute-start.5 = (bf16[4,256,768]{2,1,0:T(8,128)(2,1)S(1)}, bf16[4,256,768]{2,1,0:T(8,128)(2,1)}, u32[]{:S(2)}, u32[]{:S(2)}) collective-permute-start(bf16[4,256,768]{2,1,0:T(8,128)(2,1)S(1)} %pad_maximum_fusion.2.two_a), channel_id=1, source_target_pairs={{0,1},{1,0},{2,3},{3,2},{4,5},{5,4},{6,7},{7,6},{8,9},{9,8},{10,11... | collective-permute-start | bytes 4718600 | tf_op jit(solution)/shard_map/ppermute | solution.py:832
  148.5 19.0 %all-to-all-start.2 = ((bf16[32,64,128]{2,1,0:T(8,128)(2,1)}), bf16[32,64,128]{2,1,0:T(8,128)(2,1)}, u32[]{:S(2)}, u32[]{:S(2)}) async-start(bf16[32,64,128]{2,1,0:T(8,128)(2,1)} %get-tuple-element.85), calls=%async_computation.2 | async-start | bytes 1048576 | tf_op jit(solution)/shard_map/all_to_all | solution.py:924
  152.0 95.3 %reduce-scatter.2.cloned.1.call-start = ((), (), s32[]{:S(2)}) async-start(), calls=%async_computation.6 | async-start | bytes 184320 | tf_op jit(solution)/shard_map/reduce_scatter | solution.py:854
  152.1 12.8 %copy-start.7 = (f32[768,384]{1,0:T(8,128)S(1)}, f32[768,384]{1,0:T(8,128)}, u32[]{:S(2)}) copy-start(f32[768,384]{1,0:T(8,128)} %get-tuple-element.89) | copy-start | bytes 3538948
  152.1 12.8 %collective-permute-start.3 = (bf16[768,384]{1,0:T(8,128)(2,1)}, bf16[768,384]{1,0:T(8,128)(2,1)S(1)}, u32[]{:S(2)}, u32[]{:S(2)}) collective-permute-start(bf16[768,384]{1,0:T(8,128)(2,1)} %get-tuple-element.90), channel_id=1, source_target_pairs={{0,1},{1,0},{2,3},{3,2},{4,5},{5,4},{6,7},{7,6},{8,9},{9,8},{10,11... | collective-permute-start | bytes 1769480 | tf_op jit(solution)/shard_map/ppermute | solution.py:832
  152.2 57.2 %collective-permute-start.13 = (bf16[16,128,768]{2,1,0:T(8,128)(2,1)}, bf16[16,128,768]{2,1,0:T(8,128)(2,1)}, u32[]{:S(2)}, u32[]{:S(2)}) collective-permute-start(bf16[16,128,768]{2,1,0:T(8,128)(2,1)} %all-gather.4.cloned.1.call-done.rest_3_), channel_id=1, source_target_pairs={{0,1},{1,0},{2,3},{3,2},{4,5},{5,4},{6,7},{7,6},{8,9},{9,8},{10,11... | collective-permute-start | bytes 9437192 | tf_op jit(solution)/shard_map/ppermute | solution.py:832
  165.1 6.8 %collective-permute-start.8 = (bf16[384,384]{1,0:T(8,128)(2,1)S(1)}, bf16[384,384]{1,0:T(8,128)(2,1)S(1)}, u32[]{:S(2)}, u32[]{:S(2)}) collective-permute-start(bf16[384,384]{1,0:T(8,128)(2,1)S(1)} %fusion), channel_id=1, source_target_pairs={{0,2},{1,5},{2,0},{3,7},{4,6},{5,1},{6,4},{7,3},{8,10},{9,13},{10,... | collective-permute-start | bytes 884744 | tf_op jit(solution)/shard_map/ppermute | solution.py:832
  172.0 10.9 %collective-permute-start.9 = (bf16[192,384]{1,0:T(8,128)(2,1)S(1)}, bf16[192,384]{1,0:T(8,128)(2,1)S(1)}, u32[]{:S(2)}, u32[]{:S(2)}) collective-permute-start(bf16[192,384]{1,0:T(8,128)(2,1)S(1)} %fusion.2), channel_id=1, source_target_pairs={{0,4},{1,3},{2,6},{3,1},{4,0},{5,7},{6,2},{7,5},{8,12},{9,11},{10,... | collective-permute-start | bytes 442376 | tf_op jit(solution)/shard_map/ppermute | solution.py:832
  177.5 13.9 %collective-permute-start.10 = (bf16[384,384]{1,0:T(8,128)(2,1)S(1)}, bf16[384,384]{1,0:T(8,128)(2,1)S(1)}, u32[]{:S(2)}, u32[]{:S(2)}) collective-permute-start(bf16[384,384]{1,0:T(8,128)(2,1)S(1)} %copy-done.18), channel_id=1, source_target_pairs={{0,8},{1,9},{2,10},{3,11},{4,12},{5,13},{6,14},{7,15},{8,16},{9,17... | collective-permute-start | bytes 884744 | tf_op jit(solution)/shard_map/ppermute | solution.py:832
  179.0 21.0 %collective-permute-start.11 = (bf16[384,384]{1,0:T(8,128)(2,1)S(1)}, bf16[384,384]{1,0:T(8,128)(2,1)S(1)}, u32[]{:S(2)}, u32[]{:S(2)}) collective-permute-start(bf16[384,384]{1,0:T(8,128)(2,1)S(1)} %copy-done.17), channel_id=1, source_target_pairs={{0,16},{1,17},{2,18},{3,19},{4,20},{5,21},{6,22},{7,23},{8,24},{9,... | collective-permute-start | bytes 884744 | tf_op jit(solution)/shard_map/ppermute | solution.py:832
  181.5 18.5 %collective-permute-start.12 = (bf16[384,384]{1,0:T(8,128)(2,1)S(1)}, bf16[384,384]{1,0:T(8,128)(2,1)S(1)}, u32[]{:S(2)}, u32[]{:S(2)}) collective-permute-start(bf16[384,384]{1,0:T(8,128)(2,1)S(1)} %copy-done.16), channel_id=1, source_target_pairs={{0,24},{1,25},{2,26},{3,27},{4,28},{5,29},{6,30},{7,31},{8,0},{9,1... | collective-permute-start | bytes 884744 | tf_op jit(solution)/shard_map/ppermute | solution.py:832
  183.6 16.4 %copy-start.12 = (bf16[384,384]{1,0:T(8,128)(2,1)S(1)}, bf16[384,384]{1,0:T(8,128)(2,1)}, u32[]{:S(2)}) copy-start(bf16[384,384]{1,0:T(8,128)(2,1)} %get-tuple-element.93) | copy-start | bytes 884740
  200.1 28.5 %collective-permute-start.14 = (bf16[384,384]{1,0:T(8,128)(2,1)S(1)}, bf16[384,384]{1,0:T(8,128)(2,1)S(1)}, u32[]{:S(2)}, u32[]{:S(2)}) collective-permute-start(bf16[384,384]{1,0:T(8,128)(2,1)S(1)} %add_convert_fusion), channel_id=1, source_target_pairs={{0,8},{1,9},{2,10},{3,11},{4,12},{5,13},{6,14},{7,15},{8,16},{9,17... | collective-permute-start | bytes 884744 | tf_op jit(solution)/shard_map/ppermute | solution.py:832
  207.0 21.6 %collective-permute-start.15 = (bf16[384,384]{1,0:T(8,128)(2,1)S(1)}, bf16[384,384]{1,0:T(8,128)(2,1)S(1)}, u32[]{:S(2)}, u32[]{:S(2)}) collective-permute-start(bf16[384,384]{1,0:T(8,128)(2,1)S(1)} %add_convert_fusion), channel_id=1, source_target_pairs={{0,16},{1,17},{2,18},{3,19},{4,20},{5,21},{6,22},{7,23},{8,24},{9,... | collective-permute-start | bytes 884744 | tf_op jit(solution)/shard_map/ppermute | solution.py:832
  208.5 20.1 %collective-permute-start.16 = (bf16[384,384]{1,0:T(8,128)(2,1)S(1)}, bf16[384,384]{1,0:T(8,128)(2,1)S(1)}, u32[]{:S(2)}, u32[]{:S(2)}) collective-permute-start(bf16[384,384]{1,0:T(8,128)(2,1)S(1)} %add_convert_fusion), channel_id=1, source_target_pairs={{0,24},{1,25},{2,26},{3,27},{4,28},{5,29},{6,30},{7,31},{8,0},{9,1... | collective-permute-start | bytes 884744 | tf_op jit(solution)/shard_map/ppermute | solution.py:832
  225.0 12.0 %collective-permute-start.17 = (bf16[192,384]{1,0:T(8,128)(2,1)}, bf16[192,384]{1,0:T(8,128)(2,1)S(1)}, u32[]{:S(2)}, u32[]{:S(2)}) collective-permute-start(bf16[192,384]{1,0:T(8,128)(2,1)} %get-tuple-element.116), channel_id=1, source_target_pairs={{0,2},{1,3},{2,0},{3,1},{4,6},{5,7},{6,4},{7,5},{8,10},{9,11},{10,... | collective-permute-start | bytes 442376 | tf_op jit(solution)/shard_map/ppermute | solution.py:832
  228.6 50.5 %all-to-all-start.3 = ((bf16[32,192,128]{2,1,0:T(8,128)(2,1)}), bf16[32,192,128]{2,1,0:T(8,128)(2,1)}, u32[]{:S(2)}, u32[]{:S(2)}) async-start(bf16[32,192,128]{2,1,0:T(8,128)(2,1)} %get-tuple-element.114), calls=%async_computation.3 | async-start | bytes 3145728 | tf_op jit(solution)/shard_map/all_to_all | solution.py:924
  236.9 112.5 %all-gather.6.cloned.1.call-start = ((), (), s32[]{:S(2)}) async-start(), calls=%async_computation.7 | async-start | bytes 6082560 | tf_op jit(solution)/shard_map/all_gather | solution.py:1004
  249.0 23.5 %collective-permute-start.18 = (bf16[1536,384]{1,0:T(8,128)(2,1)S(1)}, bf16[1536,384]{1,0:T(8,128)(2,1)S(1)}, u32[]{:S(2)}, u32[]{:S(2)}) collective-permute-start(bf16[1536,384]{1,0:T(8,128)(2,1)S(1)} %pad_maximum_fusion.4), channel_id=1, source_target_pairs={{0,4},{1,3},{2,6},{3,1},{4,0},{5,7},{6,2},{7,5},{8,12},{9,11},{10,... | collective-permute-start | bytes 3538952 | tf_op jit(solution)/shard_map/ppermute | solution.py:832
  279.4 41.8 %collective-permute-start.19 = (bf16[2,1536,384]{2,1,0:T(8,128)(2,1)S(1)}, bf16[2,1536,384]{2,1,0:T(8,128)(2,1)S(1)}, u32[]{:S(2)}, u32[]{:S(2)}) collective-permute-start(bf16[2,1536,384]{2,1,0:T(8,128)(2,1)S(1)} %pad_maximum_fusion.1), channel_id=1, source_target_pairs={{0,2},{1,5},{2,0},{3,7},{4,6},{5,1},{6,4},{7,3},{8,10},{9,13},{10,... | collective-permute-start | bytes 7077896 | tf_op jit(solution)/shard_map/ppermute | solution.py:832
  323.6 16.0 %collective-permute-start.20 = (bf16[4,1536,384]{2,1,0:T(8,128)(2,1)}, bf16[4,1536,384]{2,1,0:T(8,128)(2,1)}, u32[]{:S(2)}, u32[]{:S(2)}) collective-permute-start(bf16[4,1536,384]{2,1,0:T(8,128)(2,1)} %pad_maximum_fusion.ref), channel_id=1, source_target_pairs={{0,1},{1,0},{2,3},{3,2},{4,5},{5,4},{6,7},{7,6},{8,9},{9,8},{10,11... | collective-permute-start | bytes 14155784 | tf_op jit(solution)/shard_map/ppermute | solution.py:832
  (15 other events, 95.6 us)
Sparse Core Ops, SparseCore 0:
  40.5 66.7 all-gather.3
  228.7 18.5 reduce-scatter.1
  251.2 80.9 all-gather.5
